TPU v7x, 128 devices: a whole 4x4x4 slice. The times are simulated.
128 devices in a mesh: ctx: 32 (over y, x_lo, z), fsdp: 4 (over x_hi, core).
Axes of the slice: x: 4 (x_hi: 2, x_lo: 2; x = x_hi * 2 + x_lo), y: 4, z: 4, core: 2. Of those that a mesh axis runs over, the one named last changes fastest.
Arguments:
- tokens: bfloat16 [4, 4096, 768], P('fsdp', 'ctx'), may hold values from -6 to 6
- cotangent: bfloat16 [4, 4096, 768], P('fsdp', 'ctx'), may hold values from -6 to 6
- positions: int32 [4, 4096], P('fsdp'), may hold values from 0 to 4095, as said below
- vectors: float32 [13, 768], replicated, may hold values from -1.2 to 1.6, as said below
- vectors_moment: float32 [13, 768], replicated, may hold values from -64 to 64
- vectors_second: float32 [13, 768], replicated, may hold values from 425.984 to 1638.4
- qkv_weight: float32 [768, 2304], P('fsdp'), may hold values from -0.3125 to 0.3125
- qkv_moment: float32 [768, 2304], P('fsdp'), may hold values from -40 to 40
- qkv_second: float32 [768, 2304], P('fsdp'), may hold values from 212.992 to 868.352
- dense_weight: float32 [768, 768], P('fsdp'), may hold values from -1.25 to 1.25
- dense_moment: float32 [768, 768], P('fsdp'), may hold values from -14 to 14
- dense_second: float32 [768, 768], P('fsdp'), may hold values from 19.6608 to 78.6432
- up_weight: float32 [768, 3072], P('fsdp'), may hold values from -0.21875 to 0.21875
- up_moment: float32 [768, 3072], P('fsdp'), may hold values from -24 to 24
- up_second: float32 [768, 3072], P('fsdp'), may hold values from 78.6432 to 311.296
- down_weight: float32 [3072, 768], P('fsdp'), may hold values from -0.109375 to 0.109375
- down_moment: float32 [3072, 768], P('fsdp'), may hold values from -56 to 56
- down_second: float32 [3072, 768], P('fsdp'), may hold values from 360.448 to 1474.56
Outputs:
- block_out: bfloat16 [4, 4096, 768], P('fsdp', 'ctx')
- input_grad: float32 [4, 4096, 768], P('fsdp', 'ctx')
- vectors_new: float32 [13, 768], replicated
- vectors_moment_new: float32 [13, 768], replicated
- vectors_second_new: float32 [13, 768], replicated
- qkv_new: float32 [768, 2304], P('fsdp')
- qkv_moment_new: float32 [768, 2304], P('fsdp')
- qkv_second_new: float32 [768, 2304], P('fsdp')
- dense_new: float32 [768, 768], P('fsdp')
- dense_moment_new: float32 [768, 768], P('fsdp')
- dense_second_new: float32 [768, 768], P('fsdp')
- up_new: float32 [768, 3072], P('fsdp')
- up_moment_new: float32 [768, 3072], P('fsdp')
- up_second_new: float32 [768, 3072], P('fsdp')
- down_new: float32 [3072, 768], P('fsdp')
- down_moment_new: float32 [3072, 768], P('fsdp')
- down_second_new: float32 [3072, 768], P('fsdp')
Inputs may be any that keep to these rules, and one draw needn't show every extreme that they name: Each row is a permutation of the positions of one sequence, made of blocks of 64 consecutive positions; each run of 128 stored tokens holds block j and block 63 - j for some j, in either order. `vectors`: rows 0 and 2 are gains near 1; the other rows are biases of both signs.
All inputs are finite; a program needn't handle non-finite values.
Results may differ from a plain program's by a relative error of at most 0.01.
The roundings to bfloat16 on the way count: a program that leaves them out, or rounds other values in their place, can miss the bound.
Values may be sent and summed in bfloat16 or wider, within the bound.
A program may use at most 256 MiB of HBM per device.

v0:
```python
from functools import partial
import math

import jax
import jax.numpy as jnp
from jax import lax
from jax.sharding import PartitionSpec as P

HEADS = 12
ROT = 16
STEP = 10


masked = -1e30
norm_eps = 1e-05
adam_eps = 1e-08
beta_first = 0.9
beta_second = 0.95


def angle_tables(places):
    half_rot = ROT // 2
    frequency = 10000.0 ** (-(jnp.arange(half_rot, dtype=jnp.float32) * 2.0 / ROT))
    angles = places.astype(jnp.float32)[:, None] * frequency[None, :]
    return (jnp.cos(angles), jnp.sin(angles))


def rotate(values, cos_part, sin_part):
    half_rot = cos_part.shape[-1]
    cos_wide = cos_part[:, None, :]
    sin_wide = sin_part[:, None, :]
    low_half = values[..., :half_rot]
    high_half = values[..., half_rot : 2 * half_rot]
    rest_part = values[..., 2 * half_rot :]
    return jnp.concatenate(
        [
            low_half * cos_wide - high_half * sin_wide,
            high_half * cos_wide + low_half * sin_wide,
            rest_part,
        ],
        -1,
    )


def layer_norm(inputs, gain_row, shift_row):
    centered = inputs - jnp.mean(inputs, -1, keepdims=True)
    inv_scale = lax.rsqrt(jnp.mean(centered * centered, -1, keepdims=True) + norm_eps)
    normed = centered * inv_scale
    return (normed * gain_row + shift_row, normed, inv_scale)


def norm_back(incoming, normed, inv_scale, gain_row):
    scaled = incoming * gain_row
    return inv_scale * (
        scaled
        - jnp.mean(scaled, -1, keepdims=True)
        - normed * jnp.mean(scaled * normed, -1, keepdims=True)
    )


def adamw(weight, moment, second, gradient, step_rate, decay_rate):
    moment_new = beta_first * moment + (1.0 - beta_first) * gradient
    second_new = beta_second * second + (1.0 - beta_second) * gradient * gradient
    corrected_first = moment_new / (1.0 - beta_first**STEP)
    corrected_second = second_new / (1.0 - beta_second**STEP)
    weight_new = weight - step_rate * (
        corrected_first / (jnp.sqrt(corrected_second) + adam_eps) + decay_rate * weight
    )
    return (weight_new, moment_new, second_new)


def block_scores(queries, key_block, place_block, own_places):
    scores = (
        jnp.einsum("qhd,khd->hqk", queries, key_block, preferred_element_type=jnp.float32) * 0.125
    )
    visible = place_block[None, None, :] <= own_places[None, :, None]
    return (jnp.where(visible, scores, masked), visible)


def split_blocks(keys, values, all_places):
    seq_length, head_count, head_size = keys.shape
    block_rows = math.gcd(2048, seq_length)
    block_count = seq_length // block_rows
    return (
        keys.reshape(block_count, block_rows, head_count, head_size),
        values.reshape(block_count, block_rows, head_count, head_size),
        all_places.reshape(block_count, block_rows),
    )


def attend(queries, keys, values, all_places, own_places):
    row_count, head_count, head_size = queries.shape
    key_blocks, value_blocks, place_blocks = split_blocks(keys, values, all_places)

    def total_step(carry, sliced):
        running_top, running_sum = carry
        key_block, place_block = sliced
        scores, visible = block_scores(queries, key_block, place_block, own_places)
        new_top = jnp.maximum(running_top, jnp.max(scores, -1))
        soft_weights = jnp.where(visible, jnp.exp(scores - new_top[..., None]), 0.0)
        return (
            (new_top, running_sum * jnp.exp(running_top - new_top) + jnp.sum(soft_weights, -1)),
            None,
        )

    initial = (
        jnp.full((head_count, row_count), masked, jnp.float32),
        jnp.zeros((head_count, row_count), jnp.float32),
    )
    (running_top, running_sum), _ = lax.scan(total_step, initial, (key_blocks, place_blocks))
    log_total = running_top + jnp.log(running_sum)

    def output_step(outputs, sliced):
        key_block, value_block, place_block = sliced
        scores, visible = block_scores(queries, key_block, place_block, own_places)
        soft_weights = jnp.where(visible, jnp.exp(scores - log_total[..., None]), 0.0)
        outputs = outputs + jnp.einsum(
            "hqk,khd->qhd",
            soft_weights.astype(jnp.bfloat16),
            value_block,
            preferred_element_type=jnp.float32,
        )
        return (outputs, None)

    empty = jnp.zeros((row_count, head_count, head_size), jnp.float32)
    outputs, _ = lax.scan(output_step, empty, (key_blocks, value_blocks, place_blocks))
    return (outputs, log_total)


def attend_back(queries, keys, values, all_places, own_places, log_total, grad_attn, correction):
    seq_length, head_count, head_size = keys.shape
    key_blocks, value_blocks, place_blocks = split_blocks(keys, values, all_places)
    grad_q = jnp.zeros(queries.shape, jnp.float32)
    key_parts = []
    value_parts = []
    for index in range(key_blocks.shape[0]):
        key_block = key_blocks[index]
        value_block = value_blocks[index]
        scores, visible = block_scores(queries, key_block, place_blocks[index], own_places)
        soft_weights = jnp.where(visible, jnp.exp(scores - log_total[..., None]), 0.0)
        grad_probs = jnp.einsum(
            "qhd,khd->hqk", grad_attn, value_block, preferred_element_type=jnp.float32
        )
        grad_scores = (soft_weights * (grad_probs - correction[..., None])).astype(jnp.bfloat16)
        grad_q = (
            grad_q
            + jnp.einsum("hqk,khd->qhd", grad_scores, key_block, preferred_element_type=jnp.float32)
            * 0.125
        )
        key_parts.append(
            jnp.einsum("hqk,qhd->khd", grad_scores, queries, preferred_element_type=jnp.float32)
            * 0.125
        )
        value_parts.append(
            jnp.einsum(
                "hqk,qhd->khd",
                soft_weights.astype(jnp.bfloat16),
                grad_attn,
                preferred_element_type=jnp.float32,
            )
        )
    grad_k = jnp.concatenate(key_parts, 0)
    grad_v = jnp.concatenate(value_parts, 0)
    return (
        grad_q,
        grad_k.reshape(seq_length, head_count * head_size),
        grad_v.reshape(seq_length, head_count * head_size),
    )


def body(
    tokens,
    cotangent,
    positions,
    vectors,
    vectors_moment,
    vectors_second,
    qkv_weight,
    qkv_moment,
    qkv_second,
    dense_weight,
    dense_moment,
    dense_second,
    up_weight,
    up_moment,
    up_second,
    down_weight,
    down_moment,
    down_second,
):
    inputs = tokens[0].astype(jnp.float32)
    grad_out = cotangent[0]
    row_count, model_width = inputs.shape
    head_count = HEADS
    head_size = model_width // head_count
    all_places = positions[0]
    seq_length = all_places.shape[0]
    own_places = lax.dynamic_slice_in_dim(all_places, lax.axis_index("ctx") * row_count, row_count)
    cos_part, sin_part = angle_tables(own_places)
    weights = (
        lax.all_gather(qkv_weight.astype(jnp.bfloat16), "fsdp", axis=0, tiled=True),
        lax.all_gather(dense_weight.astype(jnp.bfloat16), "fsdp", axis=0, tiled=True),
        lax.all_gather(up_weight.astype(jnp.bfloat16), "fsdp", axis=0, tiled=True),
        lax.all_gather(down_weight.astype(jnp.bfloat16), "fsdp", axis=0, tiled=True),
    )
    qkv_low, dense_low, up_low, down_low = weights
    normed_out_a, normed_a, scale_a = layer_norm(inputs, vectors[0], vectors[1])
    normed_out_b, normed_b, scale_b = layer_norm(inputs, vectors[2], vectors[3])
    ln_a = normed_out_a.astype(jnp.bfloat16)
    ln_b = normed_out_b.astype(jnp.bfloat16)
    linear = jnp.dot(ln_a, qkv_low, preferred_element_type=jnp.float32) + vectors[4:7].reshape(-1)
    query_pre = linear[:, :model_width].reshape(row_count, head_count, head_size)
    key_pre = linear[:, model_width : 2 * model_width].reshape(row_count, head_count, head_size)
    queries = rotate(query_pre, cos_part, sin_part).astype(jnp.bfloat16)
    own_keys = (
        rotate(key_pre, cos_part, sin_part).astype(jnp.bfloat16).reshape(row_count, model_width)
    )
    own_values = linear[:, 2 * model_width :].astype(jnp.bfloat16)
    key_all, value_all = (
        lax.all_gather(own_keys, "ctx", axis=0, tiled=True),
        lax.all_gather(own_values, "ctx", axis=0, tiled=True),
    )
    attended, log_total = attend(
        queries,
        key_all.reshape(seq_length, head_count, head_size),
        value_all.reshape(seq_length, head_count, head_size),
        all_places,
        own_places,
    )
    attn_low = attended.reshape(row_count, model_width).astype(jnp.bfloat16)
    hidden = jnp.dot(ln_b, up_low, preferred_element_type=jnp.float32) + vectors[8:12].reshape(-1)
    gelu_value, gelu_pull = jax.vjp(partial(jax.nn.gelu, approximate=False), hidden)
    gelu_low = gelu_value.astype(jnp.bfloat16)
    attn_out = jnp.dot(attn_low, dense_low, preferred_element_type=jnp.float32) + vectors[7]
    mlp_out = jnp.dot(gelu_low, down_low, preferred_element_type=jnp.float32) + vectors[12]
    block_out = (inputs + attn_out + mlp_out).astype(jnp.bfloat16)[None]
    qkv_back, dense_back, up_back, down_back = (
        lax.all_gather(qkv_weight.astype(jnp.bfloat16), "fsdp", axis=0, tiled=True),
        lax.all_gather(dense_weight.astype(jnp.bfloat16), "fsdp", axis=0, tiled=True),
        lax.all_gather(up_weight.astype(jnp.bfloat16), "fsdp", axis=0, tiled=True),
        lax.all_gather(down_weight.astype(jnp.bfloat16), "fsdp", axis=0, tiled=True),
    )
    key_back, value_back = (
        lax.all_gather(own_keys, "ctx", axis=0, tiled=True),
        lax.all_gather(own_values, "ctx", axis=0, tiled=True),
    )
    grad_wide = grad_out.astype(jnp.float32)
    grad_dense = jnp.einsum("td,te->de", attn_low, grad_out, preferred_element_type=jnp.float32)
    grad_down = jnp.einsum("tf,te->fe", gelu_low, grad_out, preferred_element_type=jnp.float32)
    grad_gelu = jnp.einsum("te,fe->tf", grad_out, down_back, preferred_element_type=jnp.float32)
    grad_hidden = gelu_pull(grad_gelu)[0].astype(jnp.bfloat16)
    grad_up = jnp.einsum("td,tf->df", ln_b, grad_hidden, preferred_element_type=jnp.float32)
    grad_ln_b = jnp.einsum("tf,df->td", grad_hidden, up_back, preferred_element_type=jnp.float32)
    grad_attn = (
        jnp.einsum("te,de->td", grad_out, dense_back, preferred_element_type=jnp.float32)
        .astype(jnp.bfloat16)
        .reshape(row_count, head_count, head_size)
    )
    correction = jnp.sum(grad_attn.astype(jnp.float32) * attended, -1).T
    grad_q, grad_k_all, grad_v_all = attend_back(
        queries,
        key_back.reshape(seq_length, head_count, head_size),
        value_back.reshape(seq_length, head_count, head_size),
        all_places,
        own_places,
        log_total,
        grad_attn,
        correction,
    )
    grad_k, grad_v = (
        lax.psum_scatter(grad_k_all, "ctx", scatter_dimension=0, tiled=True),
        lax.psum_scatter(grad_v_all, "ctx", scatter_dimension=0, tiled=True),
    )
    grad_query_pre = rotate(grad_q, cos_part, -sin_part).reshape(row_count, model_width)
    grad_key_pre = rotate(
        grad_k.reshape(row_count, head_count, head_size), cos_part, -sin_part
    ).reshape(row_count, model_width)
    grad_linear = jnp.concatenate([grad_query_pre, grad_key_pre, grad_v], -1).astype(jnp.bfloat16)
    grad_qkv = jnp.einsum("td,te->de", ln_a, grad_linear, preferred_element_type=jnp.float32)
    grad_ln_a = jnp.einsum("te,de->td", grad_linear, qkv_back, preferred_element_type=jnp.float32)
    input_grad = (
        grad_wide
        + norm_back(grad_ln_a, normed_a, scale_a, vectors[0])
        + norm_back(grad_ln_b, normed_b, scale_b, vectors[2])
    )
    linear_sum = jnp.sum(grad_linear.astype(jnp.float32), 0)
    hidden_sum = jnp.sum(grad_hidden.astype(jnp.float32), 0)
    output_sum = jnp.sum(grad_wide, 0)
    norm_rows = jnp.stack(
        [
            jnp.sum(grad_ln_a * normed_a, 0),
            jnp.sum(grad_ln_a, 0),
            jnp.sum(grad_ln_b * normed_b, 0),
            jnp.sum(grad_ln_b, 0),
        ]
    )
    vector_grads = jnp.concatenate(
        [
            norm_rows,
            linear_sum.reshape(3, model_width),
            output_sum[None],
            hidden_sum.reshape(4, model_width),
            output_sum[None],
        ],
        0,
    )
    vector_grads = lax.psum(vector_grads, ("ctx", "fsdp"))
    whole = lax.psum((grad_qkv, grad_dense, grad_up, grad_down), "ctx")
    reduced = (
        lax.psum_scatter(whole[0], "fsdp", scatter_dimension=0, tiled=True),
        lax.psum_scatter(whole[1], "fsdp", scatter_dimension=0, tiled=True),
        lax.psum_scatter(whole[2], "fsdp", scatter_dimension=0, tiled=True),
        lax.psum_scatter(whole[3], "fsdp", scatter_dimension=0, tiled=True),
    )
    vec_out = adamw(vectors, vectors_moment, vectors_second, vector_grads, 0.2, 0.0)
    qkv_out = adamw(qkv_weight, qkv_moment, qkv_second, reduced[0], 0.03, 0.1)
    dense_out = adamw(dense_weight, dense_moment, dense_second, reduced[1], 0.1, 0.1)
    up_out = adamw(up_weight, up_moment, up_second, reduced[2], 0.03, 0.1)
    down_out = adamw(down_weight, down_moment, down_second, reduced[3], 0.02, 0.1)
    return (
        block_out,
        input_grad[None],
        vec_out[0],
        vec_out[1],
        vec_out[2],
        qkv_out[0],
        qkv_out[1],
        qkv_out[2],
        dense_out[0],
        dense_out[1],
        dense_out[2],
        up_out[0],
        up_out[1],
        up_out[2],
        down_out[0],
        down_out[1],
        down_out[2],
    )


def solution(mesh):
    return jax.shard_map(
        body,
        mesh=mesh,
        in_specs=(
            P("fsdp", "ctx", None),
            P("fsdp", "ctx", None),
            P("fsdp", None),
            P(),
            P(),
            P(),
            P("fsdp", None),
            P("fsdp", None),
            P("fsdp", None),
            P("fsdp", None),
            P("fsdp", None),
            P("fsdp", None),
            P("fsdp", None),
            P("fsdp", None),
            P("fsdp", None),
            P("fsdp", None),
            P("fsdp", None),
            P("fsdp", None),
        ),
        out_specs=(
            P("fsdp", "ctx", None),
            P("fsdp", "ctx", None),
            P(),
            P(),
            P(),
            P("fsdp", None),
            P("fsdp", None),
            P("fsdp", None),
            P("fsdp", None),
            P("fsdp", None),
            P("fsdp", None),
            P("fsdp", None),
            P("fsdp", None),
            P("fsdp", None),
            P("fsdp", None),
            P("fsdp", None),
            P("fsdp", None),
        ),
        check_vma=False,
    )
```

profile of v0, /device:TPU:0, one launch (start us, length us, event | category | flops | bytes accessed | tf_op | source)
XLA Modules:
  0.0 1559.3 jit_solution(16196688919212535118)
XLA Ops:
  13.1 34.4 %all-gather.7.cloned.1.call-done = bf16[768,2304]{1,0:T(8,128)(2,1)} async-done(((bf16[192,2304]{1,0:T(8,128)(2,1)}), bf16[768,2304]{1,0:T(8,128)(2,1)}) %all-gather.7.cloned.1.call-update) | async-done | bytes 3538960 | tf_op jit(solution)/shard_map/all_gather | solution.py:201
  65.8 5.0 all-gather.13.cloned.1.call-done
  74.3 150.3 %all-gather.11.cloned.1.call-done = bf16[4096,768]{0,1:T(8,128)(2,1)} async-done(((bf16[128,768]{0,1:T(8,128)(2,1)}), bf16[4096,768]{0,1:T(8,128)(2,1)}) %all-gather.11.cloned.1.call-update) | async-done | bytes 6291472 | tf_op jit(solution)/shard_map/all_gather | solution.py:220
  224.6 11.4 reshape_reshape.9
  235.9 8.3 copy.57
  244.3 16.9 %while.24 = (s32[]{:T(128)}, f32[12,128]{1,0:T(8,128)S(1)}, f32[12,128]{1,0:T(8,128)S(1)}, s32[2,2048]{1,0:T(2,128)S(1)}, s32[128]{0:T(128)S(1)}, /*index=5*/bf1...) while((s32[]{:T(128)}, f32[12,128]{1,0:T(8,128)S(1)}, ...), condition=%wide.region_5.6_spmd.clone, body=%wide.region_2.5_spmd.clone.sunk | while | flops 428088832 | bytes 29399672 | solution.py:110
  244.6 4.9 fusion.182
  253.1 4.9 fusion.182
  261.1 128.9 %all-gather.9.cloned.1.call-done = bf16[4096,768]{1,0:T(8,128)(2,1)} async-done(((bf16[128,768]{1,0:T(8,128)(2,1)}), bf16[4096,768]{1,0:T(8,128)(2,1)}) %all-gather.9.cloned.1.call-update) | async-done | bytes 6291472 | tf_op jit(solution)/shard_map/all_gather | solution.py:221
  390.0 8.8 copy.54
  398.8 11.4 reshape_reshape.8
  410.2 8.4 copy.58
  418.6 40.7 %while.25 = (s32[]{:T(128)}, f32[128,12,64]{0,2,1:T(8,128)}, bf16[2,2048,12,64]{1,3,2,0:T(8,128)(2,1)}, s32[2,2048]{1,0:T(2,128)S(1)}, s32[128]{0:T(128)S(1)}, /...) while((s32[]{:T(128)}, f32[128,12,64]{0,2,1:T(8,128)}, ...), condition=%wide.region_7.8_spmd.clone, body=%wide.region_6.7_spmd.clone.sunk | while | flops 821493760 | bytes 17267332 | solution.py:126
  419.0 8.6 constant_dynamic-slice_fusion.8
  427.6 11.4 fusion.188
  439.2 8.6 constant_dynamic-slice_fusion.8
  447.8 11.5 fusion.188
  459.3 5.0 fusion.138
  464.2 4.7 copy.62
  473.8 3.5 fusion.139
  477.3 6.4 fusion.129
  483.7 8.6 multiply_convert_fusion
  492.3 4.2 multiply_bitcast_fusion
  498.7 8.2 multiply_convert_fusion.1
  509.5 3.6 multiply_bitcast_fusion.1
  513.2 10.7 pad_maximum_fusion
  524.1 10.9 fusion.60
  535.0 10.8 fusion.57
  545.8 10.8 pad_maximum_fusion.1
  561.3 8.6 multiply_convert_fusion.2
  569.9 5.7 convert_reduce_fusion
  576.5 5.1 fusion.122
  581.7 6.2 fusion.105
  587.9 6.1 fusion.142
  594.1 5.1 fusion.75
  600.0 113.9 %reduce-scatter.7.cloned.1.call-done = f32[128,768]{0,1:T(8,128)} async-done(((f32[4096,768]{0,1:T(8,128)}), f32[128,768]{0,1:T(8,128)}) %reduce-scatter.7.cloned.1.call-update) | async-done | bytes 393232 | tf_op jit(solution)/shard_map/reduce_scatter | solution.py:271
  714.8 188.3 %reduce-scatter.9.cloned.1.call-done = f32[128,768]{0,1:T(8,128)} async-done(((f32[4096,768]{0,1:T(8,128)}), f32[128,768]{0,1:T(8,128)}) %reduce-scatter.9.cloned.1.call-update) | async-done | bytes 393232 | tf_op jit(solution)/shard_map/reduce_scatter | solution.py:272
  905.2 4.7 fusion.125
  910.2 33.5 %reduce-scatter.13.cloned.1.call-done = f32[192,768]{1,0:T(8,128)} async-done(((f32[768,768]{1,0:T(8,128)}), f32[192,768]{1,0:T(8,128)}) %reduce-scatter.13.cloned.1.call-update) | async-done | bytes 589840 | tf_op jit(solution)/shard_map/reduce_scatter | solution.py:311
  943.8 87.5 %reduce-scatter.15.cloned.1.call-done = f32[192,3072]{1,0:T(8,128)} async-done(((f32[768,3072]{1,0:T(8,128)}), f32[192,3072]{1,0:T(8,128)}) %reduce-scatter.15.cloned.1.call-update) | async-done | bytes 2359312 | tf_op jit(solution)/shard_map/reduce_scatter | solution.py:312
  1031.3 87.7 %reduce-scatter.17.cloned.1.call-done = f32[768,768]{1,0:T(8,128)} async-done(((f32[3072,768]{1,0:T(8,128)}), f32[768,768]{1,0:T(8,128)}) %reduce-scatter.17.cloned.1.call-update) | async-done | bytes 2359312 | tf_op jit(solution)/shard_map/reduce_scatter | solution.py:313
  1119.0 72.7 %reduce-scatter.11.cloned.1.call-done = f32[192,2304]{1,0:T(8,128)} async-done(((f32[768,2304]{1,0:T(8,128)}), f32[192,2304]{1,0:T(8,128)}) %reduce-scatter.11.cloned.1.call-update) | async-done | bytes 1769488 | tf_op jit(solution)/shard_map/reduce_scatter | solution.py:310
  1192.8 4.1 fusion.143
  1204.4 70.0 %psum.35 = f32[13,768]{1,0:T(8,128)S(1)} all-reduce(f32[13,768]{1,0:T(8,128)S(1)} %concatenate.36), channel_id=1, replica_groups=mesh['ctx'=32,'fsdp'=4] {'ctx','fsdp'}, use_global_device_ids=true, to_apply=%region_22.23 | all-reduce | flops 9984 | bytes 79872 | tf_op jit(solution)/shard_map/psum | solution.py:307
  1275.1 257.1 %all-reduce.3.cloned.1.call-done = (f32[192,2304]{1,0:T(8,128)}, f32[192,768]{1,0:T(8,128)}, f32[192,3072]{1,0:T(8,128)}, f32[768,768]{1,0:T(8,128)}) async-done(((f32[192,2304]{1,0:T(8,128)}, f32[192,768]{1,0:T(8,128)}, f32[192,3072]{1,0:T(8,128)}, f32[768,768]{1,0:T(8,128)}), (f32[192,2304]{1,0:T(8,128)}, f32[192,768]{1,0:T(8,128)}, f32[192,3072]{1,0:T(8,128)}, ...) | async-done | bytes 7077904 | tf_op jit(solution)/shard_map/psum | solution.py:308
  1535.3 5.4 multiply_subtract_fusion.2
  1542.0 4.6 multiply_subtract_fusion.1
  1548.4 4.1 multiply_subtract_fusion
  (223 shorter events, 69.6 us)
Async XLA Ops:
  7.2 40.4 %all-gather.7.cloned.1.call-start = ((), (), s32[]{:S(2)}) async-start(), calls=%async_computation.6 | async-start | bytes 4423680 | tf_op jit(solution)/shard_map/all_gather | solution.py:201
  9.8 61.0 %all-gather.13.cloned.1.call-start = ((), (), s32[]{:S(2)}) async-start(), calls=%async_computation.9 | async-start | bytes 1474560 | tf_op jit(solution)/shard_map/all_gather | solution.py:202
  10.7 213.9 %all-gather.11.cloned.1.call-start = ((), (), s32[]{:S(2)}) async-start(), calls=%async_computation.8 | async-start | bytes 6488064 | tf_op jit(solution)/shard_map/all_gather | solution.py:220
  11.5 36.1 %copy-start.34 = (f32[768]{0:T(1024)}, f32[768]{0:T(1024)S(1)}, u32[]{:S(2)}) copy-start(f32[768]{0:T(1024)S(1)} %get-tuple-element.197) | copy-start | bytes 9220
  11.5 36.1 %copy-start.40 = (f32[768]{0:T(1024)}, f32[768]{0:T(1024)S(1)}, u32[]{:S(2)}) copy-start(f32[768]{0:T(1024)S(1)} %get-tuple-element.196) | copy-start | bytes 9220
  12.2 35.4 %copy-start.48 = (f32[128]{0:T(128)}, f32[128]{0:T(128)S(1)}, u32[]{:S(2)}) copy-start(f32[128]{0:T(128)S(1)} %broadcast_multiply_fusion.4) | copy-start | bytes 1540
  12.4 35.2 %copy-start.50 = (f32[128]{0:T(128)}, f32[128]{0:T(128)S(1)}, u32[]{:S(2)}) copy-start(f32[128]{0:T(128)S(1)} %add_rsqrt_fusion) | copy-start | bytes 1540
  13.1 43.0 %copy-start.46 = (f32[128,8]{0,1:T(8,128)}, f32[128,8]{0,1:T(8,128)S(1)}, u32[]{:S(2)}) copy-start(f32[128,8]{0,1:T(8,128)S(1)} %get-tuple-element.280) | copy-start | bytes 12292
  50.3 8.9 copy-start.6
  58.4 331.6 %all-gather.9.cloned.1.call-start = ((), (), s32[]{:S(2)}) async-start(), calls=%async_computation.7 | async-start | bytes 6488064 | tf_op jit(solution)/shard_map/all_gather | solution.py:221
  59.1 502.2 %all-gather.15.cloned.1.call-start = ((), (), s32[]{:S(2)}) async-start(), calls=%async_computation.10 | async-start | bytes 5898240 | tf_op jit(solution)/shard_map/all_gather | solution.py:203
  60.4 10.4 copy-start.16
  60.4 509.5 %all-gather.17.cloned.1.call-start = ((), (), s32[]{:S(2)}) async-start(), calls=%async_computation.11 | async-start | bytes 5898240 | tf_op jit(solution)/shard_map/all_gather | solution.py:204
  63.3 10.5 copy-start.29
  63.3 10.5 copy-start.30
  63.3 650.5 %reduce-scatter.7.cloned.1.call-start = ((), (), s32[]{:S(2)}) async-start(), calls=%async_computation.12 | async-start | bytes 12976128 | tf_op jit(solution)/shard_map/reduce_scatter | solution.py:271
  477.3 19.5 %copy-start = (bf16[2048,768]{0,1:T(8,128)(2,1)}, bf16[2048,768]{0,1:T(8,128)(2,1)S(1)}, u32[]{:S(2)}) copy-start(bf16[2048,768]{0,1:T(8,128)(2,1)S(1)} %get-tuple-element.256) | copy-start | bytes 9437188
  477.3 6.4 copy-start.13
  477.3 6.4 copy-start.33
  492.3 4.6 copy-start.1
  498.7 8.2 copy-start.3
  523.9 379.3 %reduce-scatter.9.cloned.1.call-start = ((), (), s32[]{:S(2)}) async-start(), calls=%async_computation.13 | async-start | bytes 12976128 | tf_op jit(solution)/shard_map/reduce_scatter | solution.py:272
  524.1 10.9 copy-start.32
  556.7 387.1 %reduce-scatter.13.cloned.1.call-start = ((), (), s32[]{:S(2)}) async-start(), calls=%async_computation.15 | async-start | bytes 2949120 | tf_op jit(solution)/shard_map/reduce_scatter | solution.py:311
  560.4 470.9 %reduce-scatter.15.cloned.1.call-start = ((), (), s32[]{:S(2)}) async-start(), calls=%async_computation.16 | async-start | bytes 11796480 | tf_op jit(solution)/shard_map/reduce_scatter | solution.py:312
  569.9 6.6 copy-start.42
  569.9 6.6 copy-start.49
  569.9 6.6 copy-start.51
  581.6 537.4 %reduce-scatter.17.cloned.1.call-start = ((), (), s32[]{:S(2)}) async-start(), calls=%async_computation.17 | async-start | bytes 11796480 | tf_op jit(solution)/shard_map/reduce_scatter | solution.py:313
  587.9 603.8 %reduce-scatter.11.cloned.1.call-start = ((), (), s32[]{:S(2)}) async-start(), calls=%async_computation.14 | async-start | bytes 8847360 | tf_op jit(solution)/shard_map/reduce_scatter | solution.py:310
  594.0 310.1 %copy-start.47 = (f32[128,8]{0,1:T(8,128)S(1)}, f32[128,8]{0,1:T(8,128)}, u32[]{:S(2)}) copy-start(f32[128,8]{0,1:T(8,128)} %copy-done.46) | copy-start | bytes 12292
  594.0 311.1 %copy-start.35 = (f32[768]{0:T(1024)S(1)}, f32[768]{0:T(1024)}, u32[]{:S(2)}) copy-start(f32[768]{0:T(1024)} %copy-done.34) | copy-start | bytes 9220
  594.1 311.1 %copy-start.41 = (f32[768]{0:T(1024)S(1)}, f32[768]{0:T(1024)}, u32[]{:S(2)}) copy-start(f32[768]{0:T(1024)} %copy-done.40) | copy-start | bytes 9220
  909.9 622.3 %all-reduce.3.cloned.1.call-start = ((), (), s32[]{:S(2)}) async-start(), calls=%async_computation.18 | async-start | bytes 14155776 | tf_op jit(solution)/shard_map/psum | solution.py:308
  1197.0 4.4 copy-start.12
  1202.9 71.5 %copy-start.37 = (f32[13,768]{1,0:T(8,128)S(1)}, f32[13,768]{1,0:T(8,128)}, u32[]{:S(2)}) copy-start(f32[13,768]{1,0:T(8,128)} %param.25) | copy-start | bytes 119812
  1202.9 71.5 %copy-start.44 = (f32[13,768]{1,0:T(8,128)S(1)}, f32[13,768]{1,0:T(8,128)}, u32[]{:S(2)}) copy-start(f32[13,768]{1,0:T(8,128)} %param.26) | copy-start | bytes 119812
  1203.0 71.5 %copy-start.45 = (f32[13,768]{1,0:T(8,128)S(1)}, f32[13,768]{1,0:T(8,128)}, u32[]{:S(2)}) copy-start(f32[13,768]{1,0:T(8,128)} %param.27) | copy-start | bytes 119812
  1203.0 329.3 %copy-start.19 = (f32[192,768]{1,0:T(8,128)S(1)}, f32[192,768]{1,0:T(8,128)}, u32[]{:S(2)}) copy-start(f32[192,768]{1,0:T(8,128)} %param.31) | copy-start | bytes 1769476
  1204.3 330.9 %copy-start.9 = (f32[192,2304]{1,0:T(8,128)S(1)}, f32[192,2304]{1,0:T(8,128)}, u32[]{:S(2)}) copy-start(f32[192,2304]{1,0:T(8,128)} %param.28) | copy-start | bytes 5308420
  1535.3 5.4 copy-start.7
  1535.3 5.4 copy-start.20
  1535.3 5.4 copy-start.21
  1535.3 6.7 copy-start.25
  1542.0 4.6 copy-start.8
  1542.0 4.6 copy-start.22
  1542.0 5.6 copy-start.23
  1542.0 6.3 copy-start.24
  (22 other events, 62.5 us)
Sparse Core Ops, SparseCore 0:
  10.3 37.2 all-gather.6
  49.8 20.9 all-gather.12
  72.9 151.5 all-gather.10
  226.6 163.3 all-gather.8
  392.1 41.8 all-gather.14
  436.1 40.9 all-gather.16
  524.0 189.8 reduce-scatter.6
  716.3 186.8 reduce-scatter.8
  906.3 37.3 reduce-scatter.12
  946.5 84.7 reduce-scatter.14
  1034.2 84.7 reduce-scatter.16
  1121.7 69.9 reduce-scatter.10
  1194.5 337.7 all-reduce.2
where the time goes:
time: 1560 us
  waiting for transfers between devices  1160 us (74%)
  matrix products  146 us (9%)
  local copies, waits for them, and re-layouts  102 us (7%)
  blocking collectives  70 us (4%)
  other arithmetic  65 us (4%)
    psum x1, waiting for transfers between devices, body(): whole = lax.psum((grad_qkv, grad_dense, grad_up, grad_down), 'ctx')  257 us
    reduce_scatter x1, waiting for transfers between devices, body(): lax.psum_scatter(grad_v_all, 'ctx', scatter_dimension=0, tiled=True)  188 us
    all_gather x1, waiting for transfers between devices, body(): lax.all_gather(own_keys, 'ctx', axis=0, tiled=True)  150 us
    all_gather x1, waiting for transfers between devices, body(): lax.all_gather(own_values, 'ctx', axis=0, tiled=True)  129 us
    reduce_scatter x1, waiting for transfers between devices, body(): lax.psum_scatter(grad_k_all, 'ctx', scatter_dimension=0, tiled=True)  114 us
    reduce_scatter x1, waiting for transfers between devices, body(): lax.psum_scatter(whole[3], 'fsdp', scatter_dimension=0, tiled=True)  87.7 us
    reduce_scatter x1, waiting for transfers between devices, body(): lax.psum_scatter(whole[2], 'fsdp', scatter_dimension=0, tiled=True)  87.5 us
    reduce_scatter x1, waiting for transfers between devices, body(): lax.psum_scatter(whole[0], 'fsdp', scatter_dimension=0, tiled=True)  72.7 us
  transfers between devices with their start and end apart: 13, of which 11 were waited for; matrix products, arithmetic and copies ran while one was open for 18% of the time, Pallas kernels for 0%

commit v1 on v0

v1 whole, which is shorter than its diff:
```python
import jax
import jax.numpy as jnp
from jax import lax
from jax.experimental import pallas as pl
from jax.experimental.pallas import tpu as pltpu
from jax.sharding import PartitionSpec as P

HEADS = 12
ROT = 16
STEP = 10
MESH = pl.DeviceIdType.MESH
F32 = jnp.float32
LOW = jnp.bfloat16
VMEM_LIMIT = 56 * 1024 * 1024

masked = -1e30
norm_eps = 1e-05
adam_eps = 1e-08
beta_first = 0.9
beta_second = 0.95
log2e = 1.4426950408889634


def ctx_of(y, xl, z):
    return (lax.rem(y, 4) * 2 + lax.rem(xl, 2)) * 4 + lax.rem(z, 4)


def place():
    ctx = lax.axis_index("ctx")
    fs = lax.axis_index("fsdp")
    c = lax.div(ctx, 4)
    return ctx, fs, lax.div(c, 2), lax.rem(c, 2), lax.rem(ctx, 4)


def greet(devices):
    barrier = pltpu.get_barrier_semaphore()
    for device in devices:
        pl.semaphore_signal(barrier, inc=1, device_id=device, device_id_type=MESH)
    pl.semaphore_wait(barrier, len(devices))


class Wire:
    def __init__(self, send_sem, recv_sem, local_sem):
        self.send_sem, self.recv_sem, self.local_sem = send_sem, recv_sem, local_sem
        self.sent, self.kept, self.local, self.count = [], [], 0, 0

    def send(self, src, dst, device):
        at = self.count
        self.count += 1
        copy = pltpu.make_async_remote_copy(
            src_ref=src,
            dst_ref=dst,
            send_sem=self.send_sem.at[at],
            recv_sem=self.recv_sem.at[at],
            device_id=device,
            device_id_type=MESH,
        )
        copy.start()
        self.sent.append(copy)
        return copy

    def left(self, *copies):
        for copy in copies:
            copy.wait_send()
        self.sent = [s for s in self.sent if not any(s is c for c in copies)]

    def keep(self, src, dst):
        copy = pltpu.make_async_copy(src, dst, self.local_sem.at[self.local])
        self.local += 1
        copy.start()
        self.kept.append(copy)
        return copy

    def finish(self):
        for copy in self.sent:
            copy.wait_send()
        for copy in self.kept:
            copy.wait()


def eight_peers(y, xl, z, fs):
    return [
        (ctx_of(lax.rem(y + 1, 4), xl, z), fs),
        (ctx_of(lax.rem(y + 3, 4), xl, z), fs),
        (ctx_of(y, 1 - xl, z), fs),
    ]


def erf(x):
    x = jnp.clip(x, -3.832506856900711, 3.832506856900711)
    s = x * x
    top = jnp.full_like(x, 0.00022905065861350646)
    for k in (0.0034082910107109506, 0.050955695062380861, 0.18520832239976145, 1.128379143519084):
        top = top * s + k
    low = jnp.full_like(x, -1.1791602954361697e-7)
    for k in (0.000023547966471313185, 0.0010179625278914885, 0.014070470171167667, 0.11098505178285362, 0.49746925110067538, 1.0):
        low = low * s + k
    return x * top / low


def lanes(rows, width=128):
    return lax.broadcasted_iota(jnp.int32, (rows, width), 1)


def turn(u, cos_wide, sin_wide):
    lane = lanes(u.shape[0])
    up = pltpu.roll(u, 120, 1) * jnp.where(lane < 8, -sin_wide, 0.0)
    down = pltpu.roll(u, 8, 1) * jnp.where(lane < 8, 0.0, sin_wide)
    return u * cos_wide + up + down


def angle_lanes(start, rows):
    lane = lanes(rows)
    row = lax.broadcasted_iota(jnp.int32, (rows, 128), 0)
    spot = lax.rem(row, 64)
    for i, first in enumerate(start):
        spot = spot + jnp.where(lax.div(row, 64) == i, first, 0)
    power = lax.rem(lane, 8).astype(F32) * (2.0 / ROT)
    frequency = jnp.where(lane < ROT, jnp.exp(power * -9.210340371976184), 0.0)
    angle = spot.astype(F32) * frequency
    return jnp.cos(angle), jnp.sin(angle)


class Spread:
    def __init__(self, wire, piece, out, where):
        self.wire, self.piece, self.out, self.w = wire, piece, out, where

    def around(self, slab, halves):
        w, wire = self.w, self.wire
        me = slab(w.c)
        a, b = wire.send(me, me, w.north), wire.send(me, me, w.south)
        x = wire.send(me, me, w.side)
        yield
        x.wait_recv()
        mate = slab(w.c_mate)
        p1, p2 = wire.send(mate, mate, w.north), wire.send(mate, mate, w.south)
        a.wait_recv()
        part = halves(slab(w.c_south), 0)
        h1 = wire.send(part, part, w.north)
        b.wait_recv()
        part = halves(slab(w.c_north), 1)
        h2 = wire.send(part, part, w.south)
        yield
        h1.wait_recv()
        h2.wait_recv()
        far = slab(w.c_far)
        last = wire.send(far, far, w.side)
        yield
        for copy in (p1, p2, last):
            copy.wait_recv()

    def eight_first(self):
        w, wire, out = self.w, self.wire, self.out
        width = out.shape[-1]
        own = wire.keep(self.piece, out.at[w.z, w.c])
        own.wait()
        wire.kept = [k for k in wire.kept if k is not own]
        for _ in self.around(lambda c: out.at[w.z, c], lambda r, h: r.at[:, pl.ds(h * width // 2, width // 2)]):
            yield
        mine = out.at[w.z]
        a, b = wire.send(mine, mine, w.up), wire.send(mine, mine, w.down)
        yield
        a.wait_recv()
        part = out.at[w.zm, pl.ds(0, 4)]
        h1 = wire.send(part, part, w.up)
        b.wait_recv()
        part = out.at[w.zp, pl.ds(4, 4)]
        h2 = wire.send(part, part, w.down)
        yield
        h1.wait_recv()
        h2.wait_recv()

    def ring_first(self):
        w, wire, out = self.w, self.wire, self.out
        own = wire.keep(self.piece, out.at[w.c, w.z])
        copies = [wire.send(self.piece, out.at[w.c, w.z], d) for d in (w.opposite, w.up, w.down)]
        yield
        own.wait()
        wire.kept = [k for k in wire.kept if k is not own]
        for copy in copies:
            copy.wait_recv()
        for _ in self.around(lambda c: out.at[c], lambda r, h: r.at[pl.ds(2 * h, 2)]):
            yield


class Where:
    def __init__(self):
        ctx, fs, y, xl, z = place()
        self.ctx, self.fs, self.y, self.xl, self.z = ctx, fs, y, xl, z
        self.core, self.xh = lax.rem(fs, 2), lax.div(fs, 2)
        yp, ym, yo = lax.rem(y + 1, 4), lax.rem(y + 3, 4), lax.rem(y + 2, 4)
        self.zp, self.zm, self.zo = lax.rem(z + 1, 4), lax.rem(z + 3, 4), lax.rem(z + 2, 4)
        self.c, self.c_mate = y * 2 + xl, y * 2 + 1 - xl
        self.c_north, self.c_south, self.c_far = yp * 2 + xl, ym * 2 + xl, yo * 2 + xl
        self.c_north_mate, self.c_south_mate = yp * 2 + 1 - xl, ym * 2 + 1 - xl
        self.c_far_mate = yo * 2 + 1 - xl
        self.north, self.south, self.side = eight_peers(y, xl, z, fs)
        self.up, self.down = (ctx_of(y, xl, self.zp), fs), (ctx_of(y, xl, self.zm), fs)
        self.opposite = (ctx_of(y, xl, self.zo), fs)
        self.twin = (ctx, fs + 1 - 2 * self.core)
        self.near = (ctx_of(y, 1 - xl, z), lax.rem(fs + 2, 4))
        self.plane = []
        for dh in (1, 0):
            for dy in (2, 1, 3, 0):
                for dx in (1, 0):
                    if dh or dy or dx:
                        hh = lax.rem(self.xh + dh, 2)
                        c = lax.rem(y + dy, 4) * 2 + lax.rem(xl + dx, 2)
                        self.plane.append((hh, c, (c * 4 + z, hh * 2 + self.core)))
        self.row = []
        for dh, dx in ((1, 0), (1, 1), (0, 1)):
            hh, xx = lax.rem(self.xh + dh, 2), lax.rem(xl + dx, 2)
            self.row.append((hh, xx, ((y * 2 + xx) * 4 + z, hh * 2 + self.core)))
        self.column = [(yy, (ctx_of(yy, xl, z), fs)) for yy in (yo, yp, ym)]
        self.eight = [(c, device) for hh, c, device in self.plane[8:]]


def layer_kernel(
    places, tok, cot, wqkv, wup, wdown, wdense, vec,
    or_o, ir_o, fa_o, qa_o, qb_o,
    X, G, WQ, WU, WD, WE, sq, su, sd, se, LA, LB, N, R, CS, bias,
    KVA, QGA, EC, GE, GH, SL, GU, GD, IB, SU,
    FT, FQ, FY, FX, FR, FPS,
    KP, QP0, LL, LT, raw, gap, TOP, SUM, MIX, ACC, DKV, OUT,
    F1, MA, MB, H1, H2, MF, NF, SF,
    AT, OPB, IPB, GL, GQ, VS, EP, ET, EQ, EY, EX, ER, QP, QT, QB, QR, QPS_A, QPS_B,
    ssem, rsem, lsem, wsem,
):
    w = Where()
    wire = Wire(ssem, rsem, lsem)
    ctx, fs, y, xl, z, core = w.ctx, w.fs, w.y, w.xl, w.z, w.core
    zp, zm, zo, up, down, twin, near = w.zp, w.zm, w.zo, w.up, w.down, w.twin, w.near
    other = lax.rem(fs + 2, 4)
    parity = lax.rem(z, 2)

    load_x = pltpu.make_async_copy(tok, X.at[z], wsem.at[0])
    load_x.start()
    loads_q = []
    for t in range(3):
        for i in range(3):
            at = pl.multiple_of(t * 768 + 256 * i + 128 * lax.div(z, 2), 128)
            loads_q.append(
                pltpu.make_async_copy(
                    wqkv.at[:, pl.ds(at, 128)], sq.at[:, pl.ds((3 * t + i) * 128, 128)], wsem.at[1 + 3 * t + i]
                )
            )
    for copy in loads_q:
        copy.start()
    load_g = pltpu.make_async_copy(cot, G.at[z], wsem.at[10])
    load_g.start()
    spare = jnp.minimum(lax.rem(z + fs, 4), 2)
    load_e = pltpu.make_async_copy(wdense.at[pl.ds(pl.multiple_of(spare * 64, 64), 64)], se, wsem.at[11])
    load_e.start()
    loads_u = []
    for i in range(4):
        at = pl.multiple_of(768 * i + 192 * z - 64 * parity, 128)
        loads_u.append(
            pltpu.make_async_copy(wup.at[:, pl.ds(at, 256)], su.at[:, pl.ds(256 * i, 256)], wsem.at[12 + i])
        )
    for copy in loads_u:
        copy.start()
    load_d = pltpu.make_async_copy(wdown.at[pl.ds(pl.multiple_of(z * 192, 64), 192)], sd, wsem.at[16])
    load_d.start()

    greet([up, down, w.opposite, twin] + [device for _, _, device in w.plane])

    load_x.wait()
    x_up, x_down = wire.send(X.at[z], X.at[z], up), wire.send(X.at[z], X.at[z], down)
    for copy in loads_q:
        copy.wait()

    def piece(stage, at, odd):
        return stage[:, 128 * at + 64 * odd : 128 * at + 64 * odd + 64]

    for odd in range(2):

        @pl.when(parity == odd)
        def _():
            parts = []
            for i in range(3):
                parts += [piece(sq, 3 + i, odd), piece(sq, 6 + i, odd)]
            parts += [piece(sq, i, odd) for i in range(3)] + [jnp.zeros((192, 64), F32)]
            WQ[fs] = jnp.concatenate(parts, 1).astype(LOW)

    q_near = wire.send(WQ.at[fs], WQ.at[fs], near)
    q_twin = wire.send(WQ.at[fs], WQ.at[fs], twin)
    first = lax.div(ctx, 4) * 512
    CS[0], CS[1] = angle_lanes([places[0, first + 64 * i] for i in range(8)], 512)

    def low_block(start):
        block = lax.div(places[0, start], 64)
        return block < 32, jnp.where(block < 32, block, 63 - block)

    runs = [low_block(first + 128 * i) for i in range(4)]
    row = lax.broadcasted_iota(jnp.int32, (128, 128), 0)
    for b in range(2):
        spot = jnp.where(row < 64, runs[2 * b][1], runs[2 * b + 1][1])
        QP0[b] = spot * 64 + lax.rem(row, 64)
        QP0[2 + b] = (63 - spot) * 64 + lax.rem(row, 64)
    lane = lax.broadcasted_iota(jnp.int32, (8, 256), 1)
    line = lax.broadcasted_iota(jnp.int32, (8, 256), 0)
    for c in range(8):
        spot = jnp.zeros((8, 256), jnp.int32)
        for i in range(4):
            spot = jnp.where(lax.div(lane, 64) == i, low_block(512 * c + 128 * i)[1], spot)
        KP[c] = jnp.where(line == 0, spot, 63 - spot) * 64 + lax.rem(lane, 64)

    gain_a, shift_a, gain_b, shift_b = (vec[i : i + 1, :] for i in range(4))

    def norms(zz):
        rows = pl.ds(pl.multiple_of(128 * zz, 128), 128)
        x = X[zz].astype(F32)
        centered = x - jnp.mean(x, -1, keepdims=True)
        inv = lax.rsqrt(jnp.mean(centered * centered, -1, keepdims=True) + norm_eps)
        normed = centered * inv
        N[rows, :] = normed
        R[rows, :] = jnp.broadcast_to(inv, (128, 128))
        LA[rows, :] = (normed * gain_a + shift_a).astype(LOW)
        LB[rows, :] = (normed * gain_b + shift_b).astype(LOW)

    norms(z)
    load_e.wait()
    WE[fs] = se[...].astype(LOW)
    for copy in loads_u:
        copy.wait()
    for odd in range(2):

        @pl.when(parity == odd)
        def _():
            parts = [su[:, 256 * i + 64 * odd : 256 * i + 64 * odd + 192] for i in range(4)]
            WU[fs] = jnp.concatenate(parts, 1).astype(LOW)

    load_d.wait()
    WD[fs] = sd[...].astype(LOW)
    load_g.wait()

    for zz in range(4):

        @pl.when(z == zz)
        def _():
            def head(row, i):
                return vec[row : row + 1, 64 * (zz + 4 * i) : 64 * (zz + 4 * i) + 64]

            parts = []
            for i in range(3):
                parts += [head(5, i), head(6, i)]
            parts += [head(4, i) for i in range(3)] + [jnp.zeros((1, 64), F32)]
            bias[0:1, 0:640] = jnp.concatenate(parts, 1)
            bias[1:2, :] = jnp.concatenate(
                [vec[8 + i : 9 + i, 192 * zz : 192 * zz + 192] for i in range(4)], 1
            )

    def relay(slab, from_down, from_up):
        from_down.wait_recv()
        part = slab.at[zm, pl.ds(0, 64)]
        a = wire.send(part, part, up)
        from_up.wait_recv()
        part = slab.at[zp, pl.ds(64, 64)]
        return [a, wire.send(part, part, down)]

    def forward(slab, copy):
        copy.wait_recv()
        return wire.send(slab.at[other], slab.at[other], twin)

    wire.left(x_up, x_down)
    g_up, g_down = wire.send(G.at[z], G.at[z], up), wire.send(G.at[z], G.at[z], down)
    x_far = relay(X, x_up, x_down)
    norms(zm)
    norms(zp)
    wire.left(q_near)
    e_near, e_twin = wire.send(WE.at[fs], WE.at[fs], near), wire.send(WE.at[fs], WE.at[fs], twin)
    u_near, u_twin = wire.send(WU.at[fs], WU.at[fs], near), wire.send(WU.at[fs], WU.at[fs], twin)
    q_far = forward(WQ, q_near)
    for copy in x_far:
        copy.wait_recv()
    norms(zo)
    g_far = relay(G, g_up, g_down)
    q_twin.wait_recv()
    q_far.wait_recv()
    low256 = lanes(256) < 64

    def arrange(value, i):
        a, b = value[:64], value[64:]
        return jnp.where(runs[i][0], a, b), jnp.where(runs[i][0], b, a)

    for t in range(2):
        rows = slice(256 * t, 256 * t + 256)
        linear = dot(LA[rows, :], WQ[...].reshape(768, 640)) + bias[0:1, 0:640]
        cos_wide, sin_wide = CS[0, rows, :], CS[1, rows, :]
        ab, last = linear[:, 384:512], linear[:, 512:640]
        for h, u in enumerate((ab, pltpu.roll(ab, 64, 1), last)):
            keys = turn(linear[:, 128 * h : 128 * h + 128], cos_wide, sin_wide)
            asks = jnp.where(low256, turn(u, cos_wide, sin_wide), 0.0)
            for i in (2 * t, 2 * t + 1):
                part = slice(128 * (i - 2 * t), 128 * (i - 2 * t) + 128)
                for half, value in enumerate(arrange(keys[part], i)):
                    at = 256 * half + 64 * i
                    KVA[w.c, h, at : at + 64, :] = value.astype(LOW)
                for half, value in enumerate(arrange(asks[part], i)):
                    at = 256 * half + 64 * i
                    QGA[at : at + 64, 128 * h : 128 * h + 128] = value.astype(LOW)

    spread = Spread(wire, None, None, w)

    def gather(h):
        return spread.around(lambda c: KVA.at[c, h], lambda r, half: r.at[pl.ds(256 * half, 256)])

    kv = [gather(h) for h in range(3)]
    next(kv[0])
    next(kv[2])
    e_far = forward(WE, e_near)
    for copy in g_far + [e_twin, e_far]:
        copy.wait_recv()
    EC[192:, :] = jnp.zeros((64, 768), LOW)
    for i in range(3):
        EC[64 * i : 64 * i + 64, :] = WE[i + jnp.where(i >= 3 - z, 1, 0)]
    for t in range(2):
        grad = dot_rows(G[pl.ds(2 * t, 2)].reshape(256, 768), EC[...])
        ab, last = grad[:, :128], grad[:, 128:]
        for h, u in enumerate((pltpu.roll(ab, 64, 1), ab, pltpu.roll(last, 64, 1))):
            for i in (2 * t, 2 * t + 1):
                part = slice(128 * (i - 2 * t), 128 * (i - 2 * t) + 128)
                for half, value in enumerate(arrange(u[part], i)):
                    at = slice(256 * half + 64 * i, 256 * half + 64 * i + 64)
                    col = slice(128 * h, 128 * h + 128)
                    QGA[at, col] = jnp.where(low256[:64], QGA[at, col], value.astype(LOW))

    wire.left(u_near)
    d_near, d_twin = wire.send(WD.at[fs], WD.at[fs], near), wire.send(WD.at[fs], WD.at[fs], twin)
    u_far = forward(WU, u_near)
    for copy in (u_twin, u_far):
        copy.wait_recv()

    def feed_up(t):
        rows = pl.ds(256 * t, 256)
        hidden = dot(LB[rows, :], WU[...].reshape(768, 768)) + bias[1:2, :]
        half = 0.5 + 0.5 * erf(hidden * 0.7071067811865476)
        GE[rows, :] = (hidden * half).astype(LOW)
        SL[rows, :] = half + hidden * (jnp.exp(hidden * hidden * -0.5) * 0.3989422804014327)

    down_parts = ((GD, 1, 0, 64, 64, 768), (GD, 1, 64, 128, 0, 1536))
    up_parts = ((GU, 0, 0, 128, 0, 0), (GU, 0, 128, 64, 0, 768))

    def exchange(slab, k):
        copies = []
        for h in range(2):
            at = pl.multiple_of(192 * (2 * h + 1 - core), 64)
            copies.append(wire.send(slab.at[pl.ds(at, 192)], FT.at[k, h], twin))
        return copies

    def add_pair(copies, parts):
        for copy in copies:
            copy.wait_recv()
        for slab, k, row, size, to, col in parts:
            for h in range(2):
                at = pl.multiple_of(192 * (2 * h + core) + row, 64)
                for r in range(0, size, 16):
                    total = slab[pl.ds(pl.multiple_of(at + r, 16), 16), :].astype(F32) + FT[
                        k, h, row + r : row + r + 16, :
                    ].astype(F32)
                    FQ[(to + r) // 32, h, (to + r) // 16 % 2, :, col : col + 768] = total.astype(LOW)

    feed_up(0)
    next(kv[0])
    feed_up(1)
    next(kv[1])
    d_far = forward(WD, d_near)
    for copy in (d_twin, d_far):
        copy.wait_recv()
    for t in range(2):
        rows = pl.ds(256 * t, 256)
        grad = G[2 * t : 2 * t + 2].reshape(256, 768)
        GH[rows, :] = (dot_rows(grad, WD[...].reshape(768, 768)) * SL[rows, :]).astype(LOW)
    next(kv[0])

    @pl.loop(0, 3)
    def _(j):
        at = pl.ds(pl.multiple_of(256 * j, 256), 256)
        GD[at, :] = dot_down(GE[:, at], G[...].reshape(512, 768)).astype(LOW)

    paired_down = exchange(GD, 1)
    next(kv[2])

    @pl.loop(0, 3)
    def _(j):
        at = pl.ds(pl.multiple_of(256 * j, 256), 256)
        GU[at, :] = dot_down(LB[:, at], GH[...]).astype(LOW)

    paired_up = exchange(GU, 0)
    next(kv[1])

    low = lanes(512) < 64
    same = (
        lax.broadcasted_iota(jnp.int32, (256, 256), 0) == lax.broadcasted_iota(jnp.int32, (256, 256), 1)
    )
    same = jnp.where(same, 1.0, 0.0).astype(LOW)
    deep = lax.broadcasted_iota(jnp.int32, (128, 256), 0) < 64

    meets = ((0,), (0,), (0, 1), (0, 1))
    spots = {}
    for b in range(4):
        for side in meets[b]:
            spots[b, side] = len(spots)

    def keys_of(c, h, side):
        return KVA[c, h, 256 * side : 256 * side + 256, :]

    def twice(value):
        return jnp.concatenate([value, value], 1)

    def score(h):
        for b in range(4):
            part = QGA[128 * b : 128 * b + 128, 128 * h : 128 * h + 128]
            none = jnp.zeros_like(part)
            pile = jnp.concatenate(
                [jnp.where(low256[:128], part, none), jnp.where(low256[:128], none, part)], 0
            )
            LL[b] = pile
            LT[b] = dot_rows(same[:128, :128], pile).astype(LOW)
        TOP[...] = jnp.full_like(TOP, masked)

        @pl.loop(0, 8)
        def _(c):
            for b in range(4):
                top = TOP[b]
                for side in meets[b]:
                    pair = dot_rows(LL[b], keys_of(c, h, side))
                    scores = pair[:128]
                    if b < 2 or side:
                        seen = KP[c, side : side + 1, :] <= twice(QP0[b])
                        scores = jnp.where(seen, scores, masked)
                    raw[c, spots[b, side]] = scores
                    gap[c, spots[b, side]] = pair[128:]
                    top = jnp.maximum(top, jnp.maximum(scores[:, :128], scores[:, 128:]))
                TOP[b] = top

    def weigh():
        for b in range(4):
            TOP[b] = jnp.broadcast_to(jnp.max(TOP[b], -1, keepdims=True), (128, 128))
        SUM[...] = jnp.zeros_like(SUM)
        MIX[...] = jnp.zeros_like(MIX)

        @pl.loop(0, 8)
        def _(c):
            for b in range(4):
                total, blend = SUM[b], MIX[b]
                for side in meets[b]:
                    i = spots[b, side]
                    e = jnp.exp((raw[c, i] - twice(TOP[b])) * 0.125)
                    raw[c, i] = e
                    mix = e * gap[c, i]
                    total = total + (e[:, :128] + e[:, 128:])
                    blend = blend + (mix[:, :128] + mix[:, 128:])
                SUM[b] = total
                MIX[b] = blend

    def settle(h):
        for b in range(4):
            inverse = 1.0 / jnp.sum(SUM[b], -1, keepdims=True)
            shared = jnp.sum(MIX[b], -1, keepdims=True) * inverse
            SUM[b] = jnp.broadcast_to(inverse, (128, 128))
            MIX[b] = jnp.broadcast_to(shared, (128, 128))
        ACC[...] = jnp.zeros_like(ACC)

        @pl.loop(0, 8)
        def _(c):
            grown = [None, None]
            for b in range(4):
                total = ACC[b]
                for side in meets[b]:
                    i = spots[b, side]
                    probs = raw[c, i] * twice(SUM[b])
                    slope = probs * (gap[c, i] - twice(MIX[b]))
                    pile = jnp.concatenate([slope.astype(LOW), probs.astype(LOW)], 0)
                    total = total + dot(pile, keys_of(c, h, side))
                    part = dot(LT[b], pile)
                    grown[side] = part if grown[side] is None else grown[side] + part
                ACC[b] = total
            for side, g in enumerate(grown):
                g = jnp.where(deep, g * 0.125, g).astype(LOW)
                DKV[c, h, 256 * side : 256 * side + 256, :] = dot_rows(same, g).astype(LOW)

        done = [jnp.where(low256[:128], ACC[b, :128] * 0.125, ACC[b, 128:]) for b in range(4)]
        for i in range(4):
            at = slice(64 * (i % 2), 64 * (i % 2) + 64)
            a, b = done[i // 2][at], done[2 + i // 2][at]
            at = slice(128 * h, 128 * h + 128)
            OUT[128 * i : 128 * i + 64, at] = jnp.where(runs[i][0], a, b)
            OUT[128 * i + 64 : 128 * i + 128, at] = jnp.where(runs[i][0], b, a)

    def tree(h):
        t1 = wire.send(DKV.at[w.c_far_mate, h], F1.at[h], w.side)
        t2 = wire.send(DKV.at[w.c_north_mate, h], MA.at[h], w.north)
        t3 = wire.send(DKV.at[w.c_south_mate, h], MB.at[h], w.south)
        yield
        t1.wait_recv()
        DKV[w.c_far, h] = (DKV[w.c_far, h].astype(F32) + F1[h].astype(F32)).astype(LOW)
        t4 = wire.send(DKV.at[w.c_far, h, pl.ds(0, 256)], H1.at[h], w.south)
        t5 = wire.send(DKV.at[w.c_far, h, pl.ds(256, 256)], H2.at[h], w.north)
        t2.wait_recv()
        t3.wait_recv()
        total = DKV[w.c_mate, h].astype(F32) + MA[h].astype(F32) + MB[h].astype(F32)
        DKV[w.c_mate, h] = total.astype(LOW)
        t6 = wire.send(DKV.at[w.c_mate, h], MF.at[h], w.side)
        yield
        t4.wait_recv()
        total = DKV[w.c_south, h, 0:256, :].astype(F32) + H1[h].astype(F32)
        DKV[w.c_south, h, 0:256, :] = total.astype(LOW)
        t7 = wire.send(DKV.at[w.c_south, h], NF.at[h], w.south)
        t5.wait_recv()
        total = DKV[w.c_north, h, 256:512, :].astype(F32) + H2[h].astype(F32)
        DKV[w.c_north, h, 256:512, :] = total.astype(LOW)
        t8 = wire.send(DKV.at[w.c_north, h], SF.at[h], w.north)
        yield
        for copy in (t6, t7, t8):
            copy.wait_recv()

    def add_up(parts):
        total = parts[0].astype(F32)
        for part in parts[1:]:
            total = total + part.astype(F32)
        return total.astype(LOW)

    def ladder(packet, fy, fx, fr, out):
        copies = [wire.send(packet.at[yy], fy.at[y], device) for yy, device in w.column]
        fy[y] = packet[y]
        yield
        for copy in copies:
            copy.wait_recv()
        for h in range(2):
            for i in range(2):
                fx[h, i] = add_up([fy[j, h, i] for j in range(4)])
        me = w.xh * 2 + xl
        copies = [wire.send(fx.at[hh, xx], fr.at[me], device) for hh, xx, device in w.row]
        fr[me] = fx[w.xh, xl]
        yield
        for copy in copies:
            copy.wait_recv()
        out(add_up([fr[j] for j in range(4)]))

    def drain(steps):
        for _ in steps:
            pass

    def keep_piece(total):
        FPS[...] = total

    def keep_dense(total):
        QPS_B[:, 384:768] = total

    def arrived(copies):
        for copy in copies:
            copy.wait_recv()

    def arrived(copies):
        for copy in copies:
            copy.wait_recv()

    fl = ladder(FQ, FY, FX, FR, keep_piece)
    fa = Spread(wire, FPS, fa_o, w).eight_first()
    trees = [tree(h) for h in range(3)]
    drain(kv[0])
    score(0)
    add_pair(paired_down, down_parts)
    add_pair(paired_up, up_parts)
    next(fl)
    weigh()
    next(kv[1])
    settle(0)
    next(kv[2])
    drain(kv[1])
    score(1)
    next(trees[0])
    weigh()
    next(fl)
    settle(1)
    next(trees[0])
    drain(fl)
    next(fa)
    drain(kv[2])
    score(2)
    next(fa)
    weigh()
    next(trees[1])
    next(fa)
    settle(2)
    next(trees[2])
    next(fa)

    o0, o1, o2 = (OUT[:, 128 * i : 128 * i + 128] for i in range(3))
    AT[:, :128] = jnp.where(low, pltpu.roll(o0, 64, 1), o1).astype(LOW)
    AT[:, 128:] = jnp.where(low, pltpu.roll(o2, 64, 1), 0.0).astype(LOW)
    ge = dot_down(AT[...], G[...].reshape(512, 768))
    for i in range(4):
        empty = 3 - z
        after = ge[64 * i - 64 : 64 * i] if i else ge[0:64]
        before = ge[64 * i : 64 * i + 64] if i < 3 else ge[128:192]
        slot = jnp.where(i > empty, after, before)
        slot = jnp.where(i == empty, 0.0, slot).astype(LOW)
        EP[i, 0:64, :] = slot[:, :384]
        EP[i, 64:128, :] = slot[:, 384:]
    paired_e = [wire.send(EP.at[2 * h + 1 - core], ET.at[h], twin) for h in range(2)]
    next(trees[1])
    next(trees[0])
    SU[...] = jnp.zeros_like(SU)
    for t in range(2):
        rows = pl.ds(256 * t, 256)
        back = GH[rows, :]
        grad_ln = dot_rows(back, WU[...].reshape(768, 768))
        normed = N[rows, :]
        SU[0:1, :] += jnp.sum(grad_ln * normed, 0, keepdims=True)
        SU[1:2, :] += jnp.sum(grad_ln, 0, keepdims=True)
        SU[2:3, :] += jnp.sum(back.astype(F32), 0, keepdims=True)
        IB[rows, :] = norm_back(grad_ln, normed, R[rows, 0:1], gain_b)
    next(trees[2])
    next(trees[1])
    arrived(paired_e)
    for h in range(2):
        for c in range(8):
            at = slice(16 * c, 16 * c + 16)
            EQ[c // 2, h, c % 2] = add_up([EP[2 * h + core, at, :], ET[h, at, :]])
    el = ladder(EQ, EY, EX, ER, keep_dense)
    next(el)
    for i in range(4):
        rows = slice(128 * i, 128 * i + 128)
        total = dot(GE[rows, :], WD[...].reshape(768, 768)) + dot(AT[rows, :], EC[...])
        OPB[i] = total.astype(LOW)
    ring = ((zo, w.opposite), (zp, up), (zm, down))
    o_sent = [wire.send(OPB.at[zz], or_o.at[z], device) for zz, device in ring]
    wire.keep(OPB.at[z], or_o.at[z])
    next(trees[2])

    cos_wide, sin_wide = CS[0], -CS[1]
    u0, u1, u2 = (turn(u, cos_wide, sin_wide) for u in (o0, o1, o2))
    GL[:, 384:512] = jnp.where(low, u0, pltpu.roll(u1, 64, 1)).astype(LOW)
    GL[:, 512:640] = jnp.where(low, u2, 0.0).astype(LOW)

    def own_sum(h):
        drain(trees[h])
        total = DKV[w.c, h].astype(F32) + MF[h].astype(F32) + NF[h].astype(F32) + SF[h].astype(F32)
        for i in range(4):
            a, b = total[64 * i : 64 * i + 64], total[256 + 64 * i : 320 + 64 * i]
            rows = slice(128 * i, 128 * i + 128)
            value = jnp.concatenate([jnp.where(runs[i][0], a, b), jnp.where(runs[i][0], b, a)], 0)
            value = turn(value, CS[0, rows, :], -CS[1, rows, :])
            GL[rows, 128 * h : 128 * h + 128] = value.astype(LOW)

    def project(cols):
        for t in range(2):
            rows = slice(256 * t, 256 * t + 256)
            yield rows, dot_rows(GL[rows, cols], WQ[:, :, cols].reshape(768, -1))

    def weight_part(cols):
        @pl.loop(0, 3)
        def _(j):
            at = pl.ds(pl.multiple_of(256 * j, 256), 256)
            GQ[at, cols] = dot_down(LA[:, at], GL[:, cols]).astype(LOW)

    own_sum(0)
    own_sum(1)
    for rows, value in project(slice(0, 256)):
        SL[rows, :] = value
    for rows, value in project(slice(384, 640)):
        SL[rows, :] = SL[rows, :] + value
    weight_part(slice(0, 256))
    weight_part(slice(384, 640))
    VS[...] = jnp.zeros_like(VS)

    def note(row, values):
        for j in range(values.shape[1] // 128):
            VS[6 * row + j : 6 * row + j + 1, :] = values[:, 128 * j : 128 * j + 128]

    note(2, SU[0:1, :])
    note(3, SU[1:2, :])
    note(5, SU[2:3, :])
    note(6, jnp.sum(G[z].astype(F32), 0, keepdims=True))
    next(el)
    own_sum(2)
    dots = jnp.zeros((1, 768), F32)
    plain = jnp.zeros((1, 768), F32)
    for rows, value in project(slice(256, 384)):
        grad_ln = SL[rows, :] + value
        SL[rows, :] = grad_ln
        dots = dots + jnp.sum(grad_ln * N[rows, :], 0, keepdims=True)
        plain = plain + jnp.sum(grad_ln, 0, keepdims=True)
    note(0, dots)
    note(1, plain)
    note(4, jnp.sum(GL[...].astype(F32), 0, keepdims=True))
    weight_part(slice(256, 384))
    for i in range(4):
        QP[i, :, 0:640] = GQ[192 * i : 192 * i + 128, :]
        QP[i, 0:64, 640:1024] = GQ[192 * i + 128 : 192 * i + 192, 0:384]
        QP[i, 64:128, 640:896] = GQ[192 * i + 128 : 192 * i + 192, 384:640]
        QP[i, 64:128, 896:1024] = VS[...].astype(LOW)
    paired_q = [wire.send(QP.at[2 * h + 1 - core], QT.at[h], twin) for h in range(2)]
    next(fa)
    drain(el)
    arrived(paired_q)
    for h in range(2):
        for c in range(8):
            at = slice(16 * c, 16 * c + 16)
            QB[h, c] = add_up([QP[2 * h + core, at, :], QT[h, at, :]])
    me = w.xh * 8 + w.c
    q_plane = [wire.send(QB.at[hh, c], QR.at[me], device) for hh, c, device in w.plane]
    QR[me] = QB[w.xh, w.c]
    for t in range(4):
        rows = slice(128 * t, 128 * t + 128)
        total = norm_back(SL[rows, :], N[rows, :], R[rows, 0:1], gain_a) + IB[rows, :]
        IPB[t] = total.astype(LOW)
    i_sent = [wire.send(IPB.at[zz], ir_o.at[z], device) for zz, device in ring]
    wire.keep(IPB.at[z], ir_o.at[z])
    for copy in q_plane:
        copy.wait_recv()
    total = add_up([QR[j] for j in range(16)])
    QPS_A[...] = total[:, :640]
    QPS_B[:, :384] = total[:, 640:]
    first_a = [wire.send(QPS_A, qa_o.at[z, w.c], device) for _, device in w.eight]
    first_b = [wire.send(QPS_B, qb_o.at[w.c, z], device) for _, device in ring]
    own = wire.keep(QPS_B, qb_o.at[w.c, z]), wire.keep(QPS_A, qa_o.at[z, w.c])
    for copy in own:
        copy.wait()
    wire.kept = [k for k in wire.kept if not any(k is o for o in own)]
    arrived(first_b)
    last_b = [wire.send(qb_o.at[w.c], qb_o.at[w.c], device) for _, device in w.eight]
    arrived(first_a)
    last_a = [wire.send(qa_o.at[z], qa_o.at[z], device) for _, device in ring]
    drain(fa)
    arrived(last_b + last_a)
    for copy in o_sent + i_sent:
        copy.wait_recv()
    wire.finish()


def layer(places, tok, cot, wqkv, wup, wdown, wdense, vec):
    outs = [
        ((4, 128, 768), LOW),
        ((4, 128, 768), LOW),
        ((4, 8, 16, 2304), LOW),
        ((4, 8, 16, 640), LOW),
        ((8, 4, 16, 768), LOW),
    ]
    scratch = [
        *[((4, 128, 768), LOW)] * 2,
        ((4, 192, 640), LOW),
        *[((4, 192, 768), LOW)] * 2,
        ((4, 64, 768), LOW),
        ((192, 1152), F32),
        ((192, 1024), F32),
        ((192, 768), F32),
        ((64, 768), F32),
        *[((512, 768), LOW)] * 2,
        ((512, 768), F32),
        ((512, 128), F32),
        ((2, 512, 128), F32),
        ((8, 768), F32),
        ((8, 3, 512, 128), LOW),
        ((512, 384), LOW),
        ((256, 768), LOW),
        *[((512, 768), LOW)] * 2,
        ((512, 768), F32),
        *[((768, 768), LOW)] * 2,
        ((512, 768), F32),
        ((8, 768), F32),
        ((2, 2, 192, 768), LOW),
        ((4, 2, 2, 16, 2304), LOW),
        ((4, 2, 2, 16, 2304), LOW),
        ((2, 2, 16, 2304), LOW),
        ((4, 16, 2304), LOW),
        ((16, 2304), LOW),
        ((8, 8, 256), jnp.int32),
        ((4, 128, 128), jnp.int32),
        ((4, 256, 128), LOW),
        ((4, 128, 256), LOW),
        *[((8, 6, 128, 256), F32)] * 2,
        *[((4, 128, 128), F32)] * 3,
        ((4, 256, 128), F32),
        ((8, 3, 512, 128), LOW),
        ((512, 384), F32),
        *[((3, 512, 128), LOW)] * 3,
        *[((3, 256, 128), LOW)] * 2,
        *[((3, 512, 128), LOW)] * 3,
        ((512, 256), LOW),
        *[((4, 128, 768), LOW)] * 2,
        ((512, 640), LOW),
        ((768, 640), LOW),
        ((64, 128), F32),
        ((4, 128, 384), LOW),
        ((2, 128, 384), LOW),
        ((4, 2, 2, 16, 384), LOW),
        ((4, 2, 2, 16, 384), LOW),
        ((2, 2, 16, 384), LOW),
        ((4, 16, 384), LOW),
        ((4, 128, 1024), LOW),
        ((2, 128, 1024), LOW),
        ((2, 8, 16, 1024), LOW),
        ((16, 16, 1024), LOW),
        ((16, 640), LOW),
        ((16, 768), LOW),
    ]
    anywhere = pl.BlockSpec(memory_space=pl.ANY)
    sends = 168
    return pl.pallas_call(
        layer_kernel,
        out_shape=[jax.ShapeDtypeStruct(s, d) for s, d in outs],
        in_specs=[pl.BlockSpec(memory_space=pltpu.SMEM)]
        + [anywhere] * 6
        + [pl.BlockSpec(memory_space=pltpu.VMEM)],
        out_specs=[anywhere] * len(outs),
        scratch_shapes=[pltpu.VMEM(s, d) for s, d in scratch]
        + [
            pltpu.SemaphoreType.DMA((sends,)),
            pltpu.SemaphoreType.DMA((sends,)),
            pltpu.SemaphoreType.DMA((16,)),
            pltpu.SemaphoreType.DMA((17,)),
        ],
        compiler_params=pltpu.CompilerParams(
            collective_id=0, has_side_effects=True, vmem_limit_bytes=60 * 1024 * 1024
        ),
    )(places, tok, cot, wqkv, wup, wdown, wdense, vec)


def step_kernel(
    spot, tok, cot, ors, irs, fa, qa, qb, vec, vec_m, vec_s,
    qw, qm, qs, ew, em, es, uw, um, us, dw, dm, ds,
    blk_o, inp_o, vw_o, vm_o, vs_o,
    qw_o, qm_o, qs_o, ew_o, em_o, es_o, uw_o, um_o, us_o, dw_o, dm_o, ds_o,
    TO, CO, OR, IR, FA, QA, QB, VW, VM, VS, QW, QM, QS, EW, EM, ES, UW, UM, US, DW, DM, DS,
    BL, IN, isem, osem,
):
    count = [0, 0]

    def start(src, dst, sem, which):
        copy = pltpu.make_async_copy(src, dst, sem.at[count[which]])
        count[which] += 1
        copy.start()
        return copy

    def arrive(pairs):
        return [start(a, b, isem, 0) for a, b in pairs]

    def cut_rows(pairs, at, size):
        return [(a.at[pl.ds(at, size)], b.at[pl.ds(at, size)]) for a, b in pairs]

    up, down = ((uw, UW), (um, UM), (us, US)), ((dw, DW), (dm, DM), (ds, DS))
    dense, qkv = ((ew, EW), (em, EM), (es, ES)), ((qw, QW), (qm, QM), (qs, QS))
    load_v = arrive(((vec, VW), (vec_m, VM), (vec_s, VS)))
    load_e = arrive(((qb, QB),) + dense)
    load_small = arrive(((tok, TO), (cot, CO), (ors, OR), (irs, IR)))
    load_u1 = arrive(((fa, FA), *cut_rows(up, 0, 128)))
    load_u2 = arrive(cut_rows(up, 128, 64))
    load_d1 = arrive(cut_rows(down, 0, 384))
    load_d2 = arrive(cut_rows(down, 384, 384))
    load_q = arrive(((qa, QA),) + tuple(cut_rows(qkv, 0, 128)))
    load_q2 = arrive(cut_rows(qkv, 128, 64))
    leaving = []

    def leave(pairs):
        leaving.extend(start(a, b, osem, 1) for a, b in pairs)

    def back_rows(pairs, at, size):
        leave((b.at[pl.ds(at, size)], a.at[pl.ds(at, size)]) for a, b in pairs)

    def wait(copies):
        for copy in copies:
            copy.wait()

    def update(slabs, rows, gradient, rate, decay):
        new = adamw(slabs[0][rows, :], slabs[1][rows, :], slabs[2][rows, :], gradient, rate, decay)
        for slab, value in zip(slabs, new):
            slab[rows, :] = value

    def rows_of(start_at, size=16):
        return pl.ds(pl.multiple_of(start_at, 16), size)

    def spread_up(parts):
        parts = [p.astype(F32) for p in parts]
        return jnp.concatenate([parts[z][:, 192 * i : 192 * i + 192] for i in range(4) for z in range(4)], 1)

    wait(load_v)
    wait(load_e)

    @pl.loop(0, 4)
    def _(c):
        for o in range(3):
            z = lax.rem(o + 4 - spot[0], 4)
            gradient = jnp.concatenate([QB[c, z, :, 384:768], QB[4 + c, z, :, 384:768]], 1).astype(F32)
            update((EW, EM, ES), rows_of(64 * o + 16 * c), gradient, 0.1, 0.1)

    leave(((EW, ew_o), (EM, em_o), (ES, es_o)))
    wait(load_small)
    BL[...] = (
        TO[...].astype(F32) + jnp.sum(OR[...].astype(F32), 0) + VW[7:8, :] + VW[12:13, :]
    ).astype(LOW)
    IN[...] = CO[...].astype(F32) + jnp.sum(IR[...].astype(F32), 0)
    leave(((BL, blk_o), (IN, inp_o)))
    wait(load_u1)

    @pl.loop(0, 8)
    def _(c):
        update((UW, UM, US), rows_of(16 * c), spread_up([FA[z, c, :, 0:768] for z in range(4)]), 0.03, 0.1)

    back_rows(((uw_o, UW), (um_o, UM), (us_o, US)), 0, 128)
    wait(load_u2)

    @pl.loop(0, 4)
    def _(c):
        gradient = spread_up([FA[z, c, :, 768:1536] for z in range(4)])
        update((UW, UM, US), rows_of(128 + 16 * c), gradient, 0.03, 0.1)

    back_rows(((uw_o, UW), (um_o, UM), (us_o, US)), 128, 64)

    for half, load in enumerate((load_d1, load_d2)):
        wait(load)

        @pl.loop(0, 8)
        def _(c):
            for z in (2 * half, 2 * half + 1):
                rows = rows_of(192 * z + 64 + 16 * c)
                update((DW, DM, DS), rows, FA[z, c, :, 1536:2304].astype(F32), 0.02, 0.1)

        @pl.loop(0, 4)
        def _(c):
            for z in (2 * half, 2 * half + 1):
                rows = rows_of(192 * z + 16 * c)
                update((DW, DM, DS), rows, FA[z, 4 + c, :, 768:1536].astype(F32), 0.02, 0.1)

        back_rows(((dw_o, DW), (dm_o, DM), (ds_o, DS)), 384 * half, 384)

    wait(load_q)
    low = lanes(16) < 64

    def spread_heads(groups):
        out = []
        for t in range(3):
            for i in range(3):
                for pair in range(2):
                    halves = []
                    for odd in range(2):
                        group = groups[2 * pair + odd]
                        if t == 0:
                            u, at = group[3 + i // 2], i % 2
                        else:
                            u, at = group[i], t - 1
                        halves.append(u if at == odd else pltpu.roll(u, 64, 1))
                    out.append(jnp.where(low, halves[0], halves[1]))
        return jnp.concatenate(out, 1)

    def cut(value):
        value = value.astype(F32)
        return [value[:, 128 * j : 128 * j + 128] for j in range(value.shape[1] // 128)]

    @pl.loop(0, 8)
    def _(c):
        groups = [cut(QA[z, c]) for z in range(4)]
        update((QW, QM, QS), rows_of(16 * c), spread_heads(groups), 0.03, 0.1)

    back_rows(((qw_o, QW), (qm_o, QM), (qs_o, QS)), 0, 128)
    wait(load_q2)

    @pl.loop(0, 4)
    def _(c):
        groups = [cut(QB[c, z, :, 0:384]) + cut(QB[4 + c, z, :, 0:256]) for z in range(4)]
        update((QW, QM, QS), rows_of(128 + 16 * c), spread_heads(groups), 0.03, 0.1)

    back_rows(((qw_o, QW), (qm_o, QM), (qs_o, QS)), 128, 64)

    notes = [QB[4:8, z, :, 256:384].astype(F32).reshape(64, 128) for z in range(4)]
    total = (notes[0] + notes[1]) + (notes[2] + notes[3])

    def line(values, row):
        return jnp.concatenate([values[6 * row + j : 6 * row + j + 1, :] for j in range(6)], 1)

    linear = [line(n, 4) for n in notes]
    heads = []
    for at in (lambda i: 384 + 64 * i, lambda i: 128 * i, lambda i: 128 * i + 64):
        heads.append(
            jnp.concatenate([linear[z][:, at(i) : at(i) + 64] for i in range(3) for z in range(4)], 1)
        )
    hidden = [line(n, 5) for n in notes]
    wide = [
        jnp.concatenate([hidden[z][:, 192 * i : 192 * i + 192] for z in range(4)], 1) for i in range(4)
    ]
    ends = line(total, 6)
    lines = [line(total, i) for i in range(4)] + heads + [ends] + wide + [ends]
    for i, gradient in enumerate(lines):
        row = slice(i, i + 1)
        update((VW, VM, VS), row, gradient, 0.2, 0.0)
    leave(((VW, vw_o), (VM, vm_o), (VS, vs_o)))
    wait(leaving)


def step(spot, small, parts, vectors, weights):
    anywhere = pl.BlockSpec(memory_space=pl.ANY)
    outs = [jax.ShapeDtypeStruct((128, 768), LOW), jax.ShapeDtypeStruct((128, 768), F32)]
    operands = [*small, *parts, *vectors, *weights]
    outs += [jax.ShapeDtypeStruct(v.shape, F32) for v in [*vectors, *weights]]
    return pl.pallas_call(
        step_kernel,
        out_shape=outs,
        in_specs=[pl.BlockSpec(memory_space=pltpu.SMEM)] + [anywhere] * len(operands),
        out_specs=[anywhere] * len(outs),
        scratch_shapes=[pltpu.VMEM(v.shape, v.dtype) for v in operands]
        + [pltpu.VMEM(o.shape, o.dtype) for o in outs[:2]]
        + [pltpu.SemaphoreType.DMA((40,)), pltpu.SemaphoreType.DMA((40,))],
        compiler_params=pltpu.CompilerParams(vmem_limit_bytes=VMEM_LIMIT),
    )(spot, *operands)


def norm_back(incoming, normed, inv_scale, gain_row):
    scaled = incoming * gain_row
    return inv_scale * (
        scaled
        - jnp.mean(scaled, -1, keepdims=True)
        - normed * jnp.mean(scaled * normed, -1, keepdims=True)
    )


def adamw(weight, moment, second, gradient, step_rate, decay_rate):
    moment_new = beta_first * moment + (1.0 - beta_first) * gradient
    second_new = beta_second * second + ((1.0 - beta_second) * gradient) * gradient
    size = jnp.sqrt(second_new * (1.0 / (1.0 - beta_second**STEP))) + adam_eps
    change = moment_new * (step_rate / (1.0 - beta_first**STEP)) / size
    return (weight * (1.0 - step_rate * decay_rate) - change, moment_new, second_new)


def dot(a, b):
    return jnp.dot(a, b, preferred_element_type=F32)


def dot_rows(a, b):
    return lax.dot_general(a, b, (((1,), (1,)), ((), ())), preferred_element_type=F32)


def dot_down(a, b):
    return lax.dot_general(a, b, (((0,), (0,)), ((), ())), preferred_element_type=F32)


def body(
    tokens,
    cotangent,
    positions,
    vectors,
    vectors_moment,
    vectors_second,
    qkv_weight,
    qkv_moment,
    qkv_second,
    dense_weight,
    dense_moment,
    dense_second,
    up_weight,
    up_moment,
    up_second,
    down_weight,
    down_moment,
    down_second,
):
    fs = lax.axis_index("fsdp")
    ors, irs, fa, qa, qb = layer(
        positions, tokens[0], cotangent[0], qkv_weight, up_weight, down_weight, dense_weight, vectors
    )
    block_out, input_grad, *new = step(
        fs.reshape(1).astype(jnp.int32),
        (tokens[0], cotangent[0], ors, irs),
        (fa, qa, qb),
        (vectors, vectors_moment, vectors_second),
        (
            qkv_weight,
            qkv_moment,
            qkv_second,
            dense_weight,
            dense_moment,
            dense_second,
            up_weight,
            up_moment,
            up_second,
            down_weight,
            down_moment,
            down_second,
        ),
    )
    return (block_out[None], input_grad[None], *new)


def solution(mesh):
    split = P("fsdp", None)
    act = P("fsdp", "ctx", None)
    return jax.shard_map(
        body,
        mesh=mesh,
        in_specs=(act, act, split, P(), P(), P()) + (split,) * 12,
        out_specs=(act, act, P(), P(), P()) + (split,) * 12,
        check_vma=False,
    )
```

time: 1560 us -> 158 us (0.10)
  waiting for transfers between devices: 1160 us -> 0 us
  Pallas kernels: 0 us -> 156 us
  matrix products: 146 us -> 0 us
  local copies, waits for them, and re-layouts: 102 us -> 0 us
  blocking collectives: 70 us -> 0 us
  other arithmetic: 65 us -> 0 us
    reduce_scatter x6 -> x0, waiting for transfers between devices: 584 us -> none  [the longest x1 188 us: body(): lax.psum_scatter(grad_v_all, 'ctx', scatter_dimension=0, tiled=True)]
    all_gather x6 -> x0, waiting for transfers between devices: 319 us -> none  [the longest x1 150 us: body(): lax.all_gather(own_keys, 'ctx', axis=0, tiled=True)]
    psum x1 -> x0, waiting for transfers between devices: 257 us -> none  [body(): whole = lax.psum((grad_qkv, grad_dense, grad_up, grad_down), 'ctx')]
    pallas_call x0 -> x2, Pallas kernels: none -> 156 us  [the longest x1 139 us: layer(): pl.pallas_call(layer_kernel, out_shape=[jax.ShapeDtypeStruct(s, d) for s,...]
    dot_general x26 -> x0, matrix products: 146 us -> none  [the longest x2 22.9 us: output_step(): jnp.einsum('hqk,khd->qhd', soft_weights.astype(jnp.bfloat16), value_block...]
    psum x1 -> x0, blocking collectives: 70 us -> none  [body(): vector_grads = lax.psum(vector_grads, ('ctx', 'fsdp'))]
    unnamed x116 -> x0, local copies, waits for them, and re-layouts: 27.5 us -> none
    slice x17 -> x0, local copies, waits for them, and re-layouts: 25.3 us -> none  [the longest x3 12.6 us: attend_back(): value_block = value_blocks[index]]
  transfers between devices with their start and end apart: 13 -> 0, of which waited for: 11 -> 0; matrix products, arithmetic and copies ran while one was open for 18% -> 0% of each run, Pallas kernels for 0% -> 0%
where the time goes in v1:
time: 158 us; the launch traced here: 157 us
  Pallas kernels  156 us (99%)
    pallas_call x1, Pallas kernels, layer(): pl.pallas_call(layer_kernel, out_shape=[jax.ShapeDtypeStruct(s, d) for s,...  139 us
    pallas_call x1, Pallas kernels, step(): pl.pallas_call(step_kernel, out_shape=outs, in_specs=[pl.BlockSpec(memory...  17.3 us

profile of v1, /device:TPU:0, one launch (start us, length us, event | category | flops | bytes accessed | tf_op | source)
XLA Modules:
  0.0 156.7 jit_solution(6232222442257092452)
XLA Ops:
  0.7 138.5 %shard_map.305 = (bf16[4,128,768]{2,1,0:T(8,128)(2,1)}, bf16[4,128,768]{2,1,0:T(8,128)(2,1)}, bf16[4,8,16,2304]{3,2,1,0:T(8,128)(2,1)}, bf16[4,8,16,640]{3,2,1,0:T(8,128)(2,1)}, bf16[8,4,16,768]{3,2,1,0:T(8,128)(2,1)}) custom-call(s32[1,4096]{1,0:T(1,128)} %places.1, bf16[128,768]{1,0:T(8,128)(2,1)} %bitcast.5, bf16[128,768]{1,0:T(8,128)(2,1)} %bitcast.7, ...), custom_call_target="tpu_custom_call" | custom-call | tf_op jit(solution)/shard_map/pallas_call | solution.py:902
  139.2 17.3 %shard_map.306 = (bf16[128,768]{1,0:T(8,128)(2,1)}, f32[128,768]{1,0:T(8,128)}, f32[13,768]{1,0:T(8,128)}, f32[13,768]{1,0:T(8,128)}, f32[13,768]{1,0:T(8,128)},...) custom-call(s32[1]{0:T(128)} %bitcast.spot, ...), custom_call_target="tpu_custom_call" | custom-call | tf_op jit(solution)/shard_map/pallas_call | solution.py:1097

commit v2 on v1

--- a/solution.py
+++ b/solution.py
@@ -112,10 +112,10 @@
 def angle_lanes(start, rows):
     lane = lanes(rows)
     row = lax.broadcasted_iota(jnp.int32, (rows, 128), 0)
-    spot = lax.rem(row, 64)
+    spot = row & 63
     for i, first in enumerate(start):
-        spot = spot + jnp.where(lax.div(row, 64) == i, first, 0)
-    power = lax.rem(lane, 8).astype(F32) * (2.0 / ROT)
+        spot = spot + jnp.where((row >> 6) == i, first, 0)
+    power = (lane & 7).astype(F32) * (2.0 / ROT)
     frequency = jnp.where(lane < ROT, jnp.exp(power * -9.210340371976184), 0.0)
     angle = spot.astype(F32) * frequency
     return jnp.cos(angle), jnp.sin(angle)
@@ -152,10 +152,12 @@
     def eight_first(self):
         w, wire, out = self.w, self.wire, self.out
         width = out.shape[-1]
+        cut = (width // 128 + 1) // 2 * 128
+        ends = (pl.ds(0, cut), pl.ds(cut, width - cut))
         own = wire.keep(self.piece, out.at[w.z, w.c])
         own.wait()
         wire.kept = [k for k in wire.kept if k is not own]
-        for _ in self.around(lambda c: out.at[w.z, c], lambda r, h: r.at[:, pl.ds(h * width // 2, width // 2)]):
+        for _ in self.around(lambda c: out.at[w.z, c], lambda r, h: r.at[:, ends[h]]):
             yield
         mine = out.at[w.z]
         a, b = wire.send(mine, mine, w.up), wire.send(mine, mine, w.down)
@@ -288,22 +290,22 @@
     CS[0], CS[1] = angle_lanes([places[0, first + 64 * i] for i in range(8)], 512)
 
     def low_block(start):
-        block = lax.div(places[0, start], 64)
+        block = places[0, start] >> 6
         return block < 32, jnp.where(block < 32, block, 63 - block)
 
     runs = [low_block(first + 128 * i) for i in range(4)]
     row = lax.broadcasted_iota(jnp.int32, (128, 128), 0)
     for b in range(2):
         spot = jnp.where(row < 64, runs[2 * b][1], runs[2 * b + 1][1])
-        QP0[b] = spot * 64 + lax.rem(row, 64)
-        QP0[2 + b] = (63 - spot) * 64 + lax.rem(row, 64)
+        QP0[b] = spot * 64 + (row & 63)
+        QP0[2 + b] = (63 - spot) * 64 + (row & 63)
     lane = lax.broadcasted_iota(jnp.int32, (8, 256), 1)
     line = lax.broadcasted_iota(jnp.int32, (8, 256), 0)
     for c in range(8):
         spot = jnp.zeros((8, 256), jnp.int32)
         for i in range(4):
-            spot = jnp.where(lax.div(lane, 64) == i, low_block(512 * c + 128 * i)[1], spot)
-        KP[c] = jnp.where(line == 0, spot, 63 - spot) * 64 + lax.rem(lane, 64)
+            spot = jnp.where((lane >> 6) == i, low_block(512 * c + 128 * i)[1], spot)
+        KP[c] = jnp.where(line == 0, spot, 63 - spot) * 64 + (lane & 63)
 
     gain_a, shift_a, gain_b, shift_b = (vec[i : i + 1, :] for i in range(4))
 
@@ -814,18 +816,11 @@
     total = add_up([QR[j] for j in range(16)])
     QPS_A[...] = total[:, :640]
     QPS_B[:, :384] = total[:, 640:]
-    first_a = [wire.send(QPS_A, qa_o.at[z, w.c], device) for _, device in w.eight]
-    first_b = [wire.send(QPS_B, qb_o.at[w.c, z], device) for _, device in ring]
-    own = wire.keep(QPS_B, qb_o.at[w.c, z]), wire.keep(QPS_A, qa_o.at[z, w.c])
-    for copy in own:
-        copy.wait()
-    wire.kept = [k for k in wire.kept if not any(k is o for o in own)]
-    arrived(first_b)
-    last_b = [wire.send(qb_o.at[w.c], qb_o.at[w.c], device) for _, device in w.eight]
-    arrived(first_a)
-    last_a = [wire.send(qa_o.at[z], qa_o.at[z], device) for _, device in ring]
-    drain(fa)
-    arrived(last_b + last_a)
+    qa, qb = Spread(wire, QPS_A, qa_o, w).eight_first(), Spread(wire, QPS_B, qb_o, w).ring_first()
+    for steps in (qb, qa, qb, qa, qb, qa, qb, qa, qa):
+        next(steps)
+    for steps in (fa, qb, qa):
+        drain(steps)
     for copy in o_sent + i_sent:
         copy.wait_recv()
     wire.finish()

time: 158 us -> 167 us (1.057)
  Pallas kernels: 156 us -> 164 us
    pallas_call x1, Pallas kernels: 139 us -> 146 us  [layer(): pl.pallas_call(layer_kernel, out_shape=[jax.ShapeDtypeStruct(s, d) for s,...]
where the time goes in v2:
time: 167 us; the launch traced here: 164 us
  Pallas kernels  164 us (98%)
    pallas_call x1, Pallas kernels, layer(): pl.pallas_call(layer_kernel, out_shape=[jax.ShapeDtypeStruct(s, d) for s,...  146 us
    pallas_call x1, Pallas kernels, step(): pl.pallas_call(step_kernel, out_shape=outs, in_specs=[pl.BlockSpec(memory...  17.3 us

profile of v2, /device:TPU:0, one launch (start us, length us, event | category | flops | bytes accessed | tf_op | source)
XLA Modules:
  0.0 164.4 jit_solution(2017793581158923056)
XLA Ops:
  0.7 146.3 %shard_map.305 = (bf16[4,128,768]{2,1,0:T(8,128)(2,1)}, bf16[4,128,768]{2,1,0:T(8,128)(2,1)}, bf16[4,8,16,2304]{3,2,1,0:T(8,128)(2,1)}, bf16[4,8,16,640]{3,2,1,0:T(8,128)(2,1)}, bf16[8,4,16,768]{3,2,1,0:T(8,128)(2,1)}) custom-call(s32[1,4096]{1,0:T(1,128)} %places.1, bf16[128,768]{1,0:T(8,128)(2,1)} %bitcast.5, bf16[128,768]{1,0:T(8,128)(2,1)} %bitcast.7, ...), custom_call_target="tpu_custom_call" | custom-call | tf_op jit(solution)/shard_map/pallas_call | solution.py:897
  147.0 17.3 %shard_map.306 = (bf16[128,768]{1,0:T(8,128)(2,1)}, f32[128,768]{1,0:T(8,128)}, f32[13,768]{1,0:T(8,128)}, f32[13,768]{1,0:T(8,128)}, f32[13,768]{1,0:T(8,128)},...) custom-call(s32[1]{0:T(128)} %bitcast.spot, ...), custom_call_target="tpu_custom_call" | custom-call | tf_op jit(solution)/shard_map/pallas_call | solution.py:1092

commit v3 on v2

--- a/solution.py
+++ b/solution.py
@@ -223,7 +223,7 @@
     X, G, WQ, WU, WD, WE, sq, su, sd, se, LA, LB, N, R, CS, bias,
     KVA, QGA, EC, GE, GH, SL, GU, GD, IB, SU,
     FT, FQ, FY, FX, FR, FPS,
-    KP, QP0, LL, LT, raw, gap, TOP, SUM, MIX, ACC, DKV, OUT,
+    KP, QP0, LL, LT, raw, gap, TOPS, TOP, SUM, MIX, ACC, DKV, OUT,
     F1, MA, MB, H1, H2, MF, NF, SF,
     AT, OPB, IPB, GL, GQ, VS, EP, ET, EQ, EY, EX, ER, QP, QT, QB, QR, QPS_A, QPS_B,
     ssem, rsem, lsem, wsem,
@@ -427,6 +427,7 @@
                     col = slice(128 * h, 128 * h + 128)
                     QGA[at, col] = jnp.where(low256[:64], QGA[at, col], value.astype(LOW))
 
+    next(kv[1])
     wire.left(u_near)
     d_near, d_twin = wire.send(WD.at[fs], WD.at[fs], near), wire.send(WD.at[fs], WD.at[fs], twin)
     u_far = forward(WU, u_near)
@@ -465,7 +466,6 @@
     feed_up(0)
     next(kv[0])
     feed_up(1)
-    next(kv[1])
     d_far = forward(WD, d_near)
     for copy in (d_twin, d_far):
         copy.wait_recv()
@@ -510,7 +510,7 @@
     def twice(value):
         return jnp.concatenate([value, value], 1)
 
-    def score(h):
+    def begin(h):
         for b in range(4):
             part = QGA[128 * b : 128 * b + 128, 128 * h : 128 * h + 128]
             none = jnp.zeros_like(part)
@@ -520,58 +520,59 @@
             LL[b] = pile
             LT[b] = dot_rows(same[:128, :128], pile).astype(LOW)
         TOP[...] = jnp.full_like(TOP, masked)
-
-        @pl.loop(0, 8)
+        SUM[...] = jnp.zeros_like(SUM)
+        MIX[...] = jnp.zeros_like(MIX)
+        ACC[...] = jnp.zeros_like(ACC)
+
+    def score(h, shards):
+        @pl.loop(*shards)
         def _(c):
             for b in range(4):
-                top = TOP[b]
+                old = TOP[b]
+                top = old
+                met = []
                 for side in meets[b]:
                     pair = dot_rows(LL[b], keys_of(c, h, side))
                     scores = pair[:128]
                     if b < 2 or side:
                         seen = KP[c, side : side + 1, :] <= twice(QP0[b])
                         scores = jnp.where(seen, scores, masked)
-                    raw[c, spots[b, side]] = scores
                     gap[c, spots[b, side]] = pair[128:]
                     top = jnp.maximum(top, jnp.maximum(scores[:, :128], scores[:, 128:]))
+                    met.append((spots[b, side], scores, pair[128:]))
+                fade = jnp.exp((old - top) * 0.125)
+                total, blend = SUM[b] * fade, MIX[b] * fade
+                for i, scores, grads in met:
+                    e = jnp.exp((scores - twice(top)) * 0.125)
+                    raw[c, i] = e
+                    mix = e * grads
+                    total = total + (e[:, :128] + e[:, 128:])
+                    blend = blend + (mix[:, :128] + mix[:, 128:])
                 TOP[b] = top
+                TOPS[c, b] = top
+                SUM[b] = total
+                MIX[b] = blend
 
     def weigh():
         for b in range(4):
-            TOP[b] = jnp.broadcast_to(jnp.max(TOP[b], -1, keepdims=True), (128, 128))
-        SUM[...] = jnp.zeros_like(SUM)
-        MIX[...] = jnp.zeros_like(MIX)
-
-        @pl.loop(0, 8)
-        def _(c):
-            for b in range(4):
-                total, blend = SUM[b], MIX[b]
-                for side in meets[b]:
-                    i = spots[b, side]
-                    e = jnp.exp((raw[c, i] - twice(TOP[b])) * 0.125)
-                    raw[c, i] = e
-                    mix = e * gap[c, i]
-                    total = total + (e[:, :128] + e[:, 128:])
-                    blend = blend + (mix[:, :128] + mix[:, 128:])
-                SUM[b] = total
-                MIX[b] = blend
-
-    def settle(h):
-        for b in range(4):
-            inverse = 1.0 / jnp.sum(SUM[b], -1, keepdims=True)
-            shared = jnp.sum(MIX[b], -1, keepdims=True) * inverse
+            top = jnp.max(TOP[b], -1, keepdims=True)
+            fade = jnp.exp((TOP[b] - top) * 0.125)
+            inverse = 1.0 / jnp.sum(SUM[b] * fade, -1, keepdims=True)
+            shared = jnp.sum(MIX[b] * fade, -1, keepdims=True) * inverse
+            TOP[b] = jnp.broadcast_to(top, (128, 128))
             SUM[b] = jnp.broadcast_to(inverse, (128, 128))
             MIX[b] = jnp.broadcast_to(shared, (128, 128))
-        ACC[...] = jnp.zeros_like(ACC)
-
-        @pl.loop(0, 8)
+
+    def settle(h, shards):
+        @pl.loop(*shards)
         def _(c):
             grown = [None, None]
             for b in range(4):
                 total = ACC[b]
+                share = twice(jnp.exp((TOPS[c, b] - TOP[b]) * 0.125) * SUM[b])
                 for side in meets[b]:
                     i = spots[b, side]
-                    probs = raw[c, i] * twice(SUM[b])
+                    probs = raw[c, i] * share
                     slope = probs * (gap[c, i] - twice(MIX[b]))
                     pile = jnp.concatenate([slope.astype(LOW), probs.astype(LOW)], 0)
                     total = total + dot(pile, keys_of(c, h, side))
@@ -582,6 +583,7 @@
                 g = jnp.where(deep, g * 0.125, g).astype(LOW)
                 DKV[c, h, 256 * side : 256 * side + 256, :] = dot_rows(same, g).astype(LOW)
 
+    def finish(h):
         done = [jnp.where(low256[:128], ACC[b, :128] * 0.125, ACC[b, 128:]) for b in range(4)]
         for i in range(4):
             at = slice(64 * (i % 2), 64 * (i % 2) + 64)
@@ -661,33 +663,48 @@
     fl = ladder(FQ, FY, FX, FR, keep_piece)
     fa = Spread(wire, FPS, fa_o, w).eight_first()
     trees = [tree(h) for h in range(3)]
+    early, late = (0, 4), (4, 8)
     drain(kv[0])
-    score(0)
+    begin(0)
+    score(0, early)
+    score(0, late)
+    next(kv[1])
     add_pair(paired_down, down_parts)
     add_pair(paired_up, up_parts)
     next(fl)
     weigh()
-    next(kv[1])
-    settle(0)
+    settle(0, early)
+    settle(0, late)
+    finish(0)
+    drain(kv[1])
+    begin(1)
+    score(1, early)
     next(kv[2])
-    drain(kv[1])
-    score(1)
+    score(1, late)
     next(trees[0])
     weigh()
+    settle(1, early)
     next(fl)
-    settle(1)
+    settle(1, late)
+    finish(1)
     next(trees[0])
     drain(fl)
     next(fa)
     drain(kv[2])
-    score(2)
+    begin(2)
+    score(2, early)
+    next(trees[1])
+    next(fa)
+    score(2, late)
+    next(trees[0])
     next(fa)
     weigh()
+    settle(2, early)
     next(trees[1])
     next(fa)
-    settle(2)
+    settle(2, late)
     next(trees[2])
-    next(fa)
+    finish(2)
 
     o0, o1, o2 = (OUT[:, 128 * i : 128 * i + 128] for i in range(3))
     AT[:, :128] = jnp.where(low, pltpu.roll(o0, 64, 1), o1).astype(LOW)
@@ -703,7 +720,6 @@
         EP[i, 64:128, :] = slot[:, 384:]
     paired_e = [wire.send(EP.at[2 * h + 1 - core], ET.at[h], twin) for h in range(2)]
     next(trees[1])
-    next(trees[0])
     SU[...] = jnp.zeros_like(SU)
     for t in range(2):
         rows = pl.ds(256 * t, 256)
@@ -715,7 +731,6 @@
         SU[2:3, :] += jnp.sum(back.astype(F32), 0, keepdims=True)
         IB[rows, :] = norm_back(grad_ln, normed, R[rows, 0:1], gain_b)
     next(trees[2])
-    next(trees[1])
     arrived(paired_e)
     for h in range(2):
         for c in range(8):
@@ -816,11 +831,18 @@
     total = add_up([QR[j] for j in range(16)])
     QPS_A[...] = total[:, :640]
     QPS_B[:, :384] = total[:, 640:]
-    qa, qb = Spread(wire, QPS_A, qa_o, w).eight_first(), Spread(wire, QPS_B, qb_o, w).ring_first()
-    for steps in (qb, qa, qb, qa, qb, qa, qb, qa, qa):
-        next(steps)
-    for steps in (fa, qb, qa):
-        drain(steps)
+    first_a = [wire.send(QPS_A, qa_o.at[z, w.c], device) for _, device in w.eight]
+    first_b = [wire.send(QPS_B, qb_o.at[w.c, z], device) for _, device in ring]
+    own = wire.keep(QPS_B, qb_o.at[w.c, z]), wire.keep(QPS_A, qa_o.at[z, w.c])
+    for copy in own:
+        copy.wait()
+    wire.kept = [k for k in wire.kept if not any(k is o for o in own)]
+    arrived(first_b)
+    last_b = [wire.send(qb_o.at[w.c], qb_o.at[w.c], device) for _, device in w.eight]
+    arrived(first_a)
+    last_a = [wire.send(qa_o.at[z], qa_o.at[z], device) for _, device in ring]
+    drain(fa)
+    arrived(last_b + last_a)
     for copy in o_sent + i_sent:
         copy.wait_recv()
     wire.finish()
@@ -867,6 +889,7 @@
         ((4, 256, 128), LOW),
         ((4, 128, 256), LOW),
         *[((8, 6, 128, 256), F32)] * 2,
+        ((8, 4, 128, 128), F32),
         *[((4, 128, 128), F32)] * 3,
         ((4, 256, 128), F32),
         ((8, 3, 512, 128), LOW),

time: 167 us -> 151 us (0.904); the launches traced: 164 us -> 150 us
  Pallas kernels: 164 us -> 150 us
    pallas_call x1, Pallas kernels: 146 us -> 132 us  [layer(): pl.pallas_call(layer_kernel, out_shape=[jax.ShapeDtypeStruct(s, d) for s,...]
where the time goes in v3:
time: 151 us; the launch traced here: 150 us
  Pallas kernels  150 us (99%)
    pallas_call x1, Pallas kernels, layer(): pl.pallas_call(layer_kernel, out_shape=[jax.ShapeDtypeStruct(s, d) for s,...  132 us
    pallas_call x1, Pallas kernels, step(): pl.pallas_call(step_kernel, out_shape=outs, in_specs=[pl.BlockSpec(memory...  17.3 us

profile of v3, /device:TPU:0, one launch (start us, length us, event | category | flops | bytes accessed | tf_op | source)
XLA Modules:
  0.0 150.4 jit_solution(10384483587707633150)
XLA Ops:
  0.7 132.3 %shard_map.305 = (bf16[4,128,768]{2,1,0:T(8,128)(2,1)}, bf16[4,128,768]{2,1,0:T(8,128)(2,1)}, bf16[4,8,16,2304]{3,2,1,0:T(8,128)(2,1)}, bf16[4,8,16,640]{3,2,1,0:T(8,128)(2,1)}, bf16[8,4,16,768]{3,2,1,0:T(8,128)(2,1)}) custom-call(s32[1,4096]{1,0:T(1,128)} %places.1, bf16[128,768]{1,0:T(8,128)(2,1)} %bitcast.5, bf16[128,768]{1,0:T(8,128)(2,1)} %bitcast.7, ...), custom_call_target="tpu_custom_call" | custom-call | tf_op jit(solution)/shard_map/pallas_call | solution.py:920
  133.0 17.3 %shard_map.306 = (bf16[128,768]{1,0:T(8,128)(2,1)}, f32[128,768]{1,0:T(8,128)}, f32[13,768]{1,0:T(8,128)}, f32[13,768]{1,0:T(8,128)}, f32[13,768]{1,0:T(8,128)},...) custom-call(s32[1]{0:T(128)} %bitcast.spot, ...), custom_call_target="tpu_custom_call" | custom-call | tf_op jit(solution)/shard_map/pallas_call | solution.py:1115

commit v4 on v3

--- a/solution.py
+++ b/solution.py
@@ -810,8 +810,6 @@
         QP[i, 64:128, 640:896] = GQ[192 * i + 128 : 192 * i + 192, 384:640]
         QP[i, 64:128, 896:1024] = VS[...].astype(LOW)
     paired_q = [wire.send(QP.at[2 * h + 1 - core], QT.at[h], twin) for h in range(2)]
-    next(fa)
-    drain(el)
     arrived(paired_q)
     for h in range(2):
         for c in range(8):
@@ -826,6 +824,8 @@
         IPB[t] = total.astype(LOW)
     i_sent = [wire.send(IPB.at[zz], ir_o.at[z], device) for zz, device in ring]
     wire.keep(IPB.at[z], ir_o.at[z])
+    next(fa)
+    drain(el)
     for copy in q_plane:
         copy.wait_recv()
     total = add_up([QR[j] for j in range(16)])

time: 151 us -> 155 us (1.026)
  Pallas kernels: 150 us -> 153 us
    pallas_call x1, Pallas kernels: 132 us -> 136 us  [layer(): pl.pallas_call(layer_kernel, out_shape=[jax.ShapeDtypeStruct(s, d) for s,...]
where the time goes in v4:
time: 155 us; the launch traced here: 154 us
  Pallas kernels  153 us (99%)
    pallas_call x1, Pallas kernels, layer(): pl.pallas_call(layer_kernel, out_shape=[jax.ShapeDtypeStruct(s, d) for s,...  136 us
    pallas_call x1, Pallas kernels, step(): pl.pallas_call(step_kernel, out_shape=outs, in_specs=[pl.BlockSpec(memory...  17.3 us

profile of v4, /device:TPU:0, one launch (start us, length us, event | category | flops | bytes accessed | tf_op | source)
XLA Modules:
  0.0 154.0 jit_solution(10619619442896851033)
XLA Ops:
  0.7 135.9 %shard_map.305 = (bf16[4,128,768]{2,1,0:T(8,128)(2,1)}, bf16[4,128,768]{2,1,0:T(8,128)(2,1)}, bf16[4,8,16,2304]{3,2,1,0:T(8,128)(2,1)}, bf16[4,8,16,640]{3,2,1,0:T(8,128)(2,1)}, bf16[8,4,16,768]{3,2,1,0:T(8,128)(2,1)}) custom-call(s32[1,4096]{1,0:T(1,128)} %places.1, bf16[128,768]{1,0:T(8,128)(2,1)} %bitcast.5, bf16[128,768]{1,0:T(8,128)(2,1)} %bitcast.7, ...), custom_call_target="tpu_custom_call" | custom-call | tf_op jit(solution)/shard_map/pallas_call | solution.py:920
  136.6 17.3 %shard_map.306 = (bf16[128,768]{1,0:T(8,128)(2,1)}, f32[128,768]{1,0:T(8,128)}, f32[13,768]{1,0:T(8,128)}, f32[13,768]{1,0:T(8,128)}, f32[13,768]{1,0:T(8,128)},...) custom-call(s32[1]{0:T(128)} %bitcast.spot, ...), custom_call_target="tpu_custom_call" | custom-call | tf_op jit(solution)/shard_map/pallas_call | solution.py:1115
